TPU v7x, 32 devices: a whole 2x2x4 slice. The times are simulated.
32 devices in a mesh: groups: 1, fac: 32 (over z, y, x, core).
Axes of the slice: x: 2, y: 2, z: 4, core: 2. Of those that a mesh axis runs over, the one named last changes fastest.
Arguments:
- sky_image: float32 [64, 96, 4096], P(('groups', 'fac')), may hold values from 0 to 18, as said below
- measured_real: float32 [64, 96, 4096], P(('groups', 'fac')), may hold values from -6 to 6
- measured_imaginary: float32 [64, 96, 4096], P(('groups', 'fac')), may hold values from -6 to 6
- sampling_mask: int32 [64, 96, 4096], P(('groups', 'fac')), may hold values 0 or 1
- dual_field: float32 [64, 96, 4096], P('groups', None, 'fac'), may hold values from -6 to 6
Outputs:
- next_image: float32 [64, 96, 4096], P(('groups', 'fac'))
- next_dual: float32 [64, 96, 4096], P('groups', None, 'fac')
Inputs may be any that keep to these rules, and one draw needn't show every extreme that they name: `sky_image`: non-negative sky brightness.
All inputs are finite; a program needn't handle non-finite values. No bound on the sum of `sampling_mask` on one device may be relied on, other than what follows from the above.
Results may differ from a plain program's by a relative error of at most 0.00012.
Values sent between devices are 32-bit elements; how exact they have to be, the bound alone decides.
A program may use at most 192 MiB of HBM per device.

v0:
```python
import jax
import jax.numpy as jnp
import numpy as np
from jax import lax
from jax.sharding import PartitionSpec as P

LEVELS = 4


low_pass = (
    0.2303778133088964,
    0.7148465705529155,
    0.6308807679298587,
    -0.0279837694168599,
    -0.1870348117190931,
    0.0308413818355607,
    0.0328830116668852,
    -0.010597401785069,
)
high_pass = tuple(((-1) ** tap_index * low_pass[7 - tap_index] for tap_index in range(8)))
primal_step = 0.6
dual_step = 0.8
ball_radius = 12.0
precise = lax.Precision.HIGHEST


def contract(pattern, left_side, right_side):
    return jnp.einsum(
        pattern, left_side, right_side, precision=precise, preferred_element_type=jnp.float32
    )


def fourier_table(length, direction):
    sample_grid = np.arange(length)
    angles = 2.0 * np.pi * (np.outer(sample_grid, sample_grid) % length) / length
    factor = 1.0 / np.sqrt(length)
    return (
        jnp.asarray(np.cos(angles) * factor, jnp.float32),
        jnp.asarray(direction * np.sin(angles) * factor, jnp.float32),
    )


def twist_table(inner_size, outer_size, length, direction):
    angles = (
        2.0
        * np.pi
        * (np.arange(inner_size)[:, None] * np.arange(outer_size)[None, :] % length)
        / length
    )
    return (
        jnp.asarray(np.cos(angles), jnp.float32),
        jnp.asarray(direction * np.sin(angles), jnp.float32),
    )


def complex_step(real_part, imag_part, pattern, matrix):
    if imag_part is None:
        return (contract(pattern, real_part, matrix[0]), contract(pattern, real_part, matrix[1]))
    return (
        contract(pattern, real_part, matrix[0]) - contract(pattern, imag_part, matrix[1]),
        contract(pattern, real_part, matrix[1]) + contract(pattern, imag_part, matrix[0]),
    )


def data_gradient(sky_image, measured_real, measured_imaginary, sampling_mask):
    channels, row_count, column_count = sky_image.shape
    outer_size = 64
    inner_size = column_count // outer_size
    sample_grid = sky_image.reshape(channels, row_count, inner_size, outer_size)
    real_part, imag_part = complex_step(
        sample_grid, None, "crba,rs->csba", fourier_table(row_count, -1.0)
    )
    real_part, imag_part = complex_step(
        real_part, imag_part, "csba,bk->cska", fourier_table(inner_size, -1.0)
    )
    twist_real, twist_imag = twist_table(inner_size, outer_size, column_count, -1.0)
    real_part, imag_part = (
        real_part * twist_real - imag_part * twist_imag,
        real_part * twist_imag + imag_part * twist_real,
    )
    real_part, imag_part = complex_step(
        real_part, imag_part, "cska,aj->csjk", fourier_table(outer_size, -1.0)
    )
    weights = sampling_mask.astype(jnp.float32)
    real_part = weights * (real_part.reshape(channels, row_count, column_count) - measured_real)
    imag_part = weights * (
        imag_part.reshape(channels, row_count, column_count) - measured_imaginary
    )
    real_part = real_part.reshape(channels, row_count, outer_size, inner_size)
    imag_part = imag_part.reshape(channels, row_count, outer_size, inner_size)
    real_part, imag_part = complex_step(
        real_part, imag_part, "csjk,ja->cska", fourier_table(outer_size, 1.0)
    )
    twist_real, twist_imag = twist_table(inner_size, outer_size, column_count, 1.0)
    real_part, imag_part = (
        real_part * twist_real - imag_part * twist_imag,
        real_part * twist_imag + imag_part * twist_real,
    )
    real_part, imag_part = complex_step(
        real_part, imag_part, "cska,kb->csba", fourier_table(inner_size, 1.0)
    )
    row_real, row_imag = fourier_table(row_count, 1.0)
    result = contract("csba,sr->crba", real_part, row_real) - contract(
        "csba,sr->crba", imag_part, row_imag
    )
    return result.reshape(channels, row_count, column_count)


def row_matrix(length):
    current = np.eye(length)
    details = []
    for level_index in range(LEVELS):
        width_now = current.shape[0]
        half_size = width_now // 2
        lower = np.zeros((half_size, width_now))
        upper = np.zeros((half_size, width_now))
        for target in range(half_size):
            for tap_index in range(8):
                lower[target, (2 * target + tap_index) % width_now] += low_pass[tap_index]
                upper[target, (2 * target + tap_index) % width_now] += high_pass[tap_index]
        details.insert(0, upper @ current)
        current = lower @ current
    return jnp.asarray(np.concatenate([current] + details, 0), jnp.float32)


def analysis_step(length):
    half_size = length // 2
    matrix = np.zeros((length + 6, length))
    for target in range(half_size):
        for tap_index in range(8):
            matrix[2 * target + tap_index, target] += low_pass[tap_index]
            matrix[2 * target + tap_index, half_size + target] += high_pass[tap_index]
    return jnp.asarray(matrix, jnp.float32)


def synthesis_step(length):
    matrix = np.zeros((2 * (length + 3), 2 * length))
    for source in range(length):
        for parity in range(2):
            for back_step in range(4):
                matrix[source - back_step + 3, 2 * source + parity] += low_pass[
                    parity + 2 * back_step
                ]
                matrix[length + 3 + source - back_step + 3, 2 * source + parity] += high_pass[
                    parity + 2 * back_step
                ]
    return jnp.asarray(matrix, jnp.float32)


def column_analysis(values, right_rim):
    coarse = values
    details = []
    for level_index in range(LEVELS):
        length = coarse.shape[-1]
        extended = jnp.concatenate([coarse, right_rim(coarse[..., :6])], -1)
        halves = contract("...m,mk->...k", extended, analysis_step(length))
        details.insert(0, halves[..., length // 2 :])
        coarse = halves[..., : length // 2]
    return jnp.concatenate([coarse] + details, -1)


def column_synthesis(coefficients, left_rim):
    length = coefficients.shape[-1] >> LEVELS
    coarse = coefficients[..., :length]
    offset = length
    for level_index in range(LEVELS):
        detail = coefficients[..., offset : offset + length]
        coarse_edge, detail_edge = left_rim(coarse[..., -3:], detail[..., -3:])
        extended = jnp.concatenate([coarse_edge, coarse, detail_edge, detail], -1)
        coarse = contract("...m,mk->...k", extended, synthesis_step(length))
        offset = offset + length
        length = length * 2
    return coarse


def right_within(edge_cols):
    return jnp.roll(edge_cols, -1, axis=-2)


def left_within(coarse_edge, detail_edge):
    return (jnp.roll(coarse_edge, 1, axis=-2), jnp.roll(detail_edge, 1, axis=-2))


def shards(sky_image, measured_real, measured_imaginary, sampling_mask, dual_field):
    channels, row_count, column_count = sky_image.shape
    rows_table = row_matrix(row_count)
    gradient = data_gradient(sky_image, measured_real, measured_imaginary, sampling_mask)
    facet_count = lax.axis_size("fac")
    facet_width = column_count // facet_count
    local_dual = lax.all_to_all(dual_field, "fac", split_axis=0, concat_axis=2, tiled=True)
    coefficients = local_dual.reshape(channels, row_count, facet_count, facet_width)
    prior_term = column_synthesis(coefficients, left_within).reshape(
        channels, row_count, column_count
    )
    prior_term = contract("sr,csn->crn", rows_table, prior_term)
    next_image = jnp.maximum(sky_image - primal_step * (gradient + prior_term), 0.0)
    analysed = contract("rs,csn->crn", rows_table, 2.0 * next_image - sky_image)
    analysed = column_analysis(
        analysed.reshape(channels, row_count, facet_count, facet_width), right_within
    )
    lifted = local_dual + dual_step * analysed.reshape(channels, row_count, column_count)
    summed = lax.psum(jnp.sum(lifted * lifted, axis=0), "fac")
    shrunk = lifted / jnp.maximum(1.0, jnp.sqrt(summed) / ball_radius)
    next_dual = lax.all_to_all(shrunk, "fac", split_axis=2, concat_axis=0, tiled=True)
    return (next_image, next_dual)


def solution(mesh):
    return jax.shard_map(
        shards,
        mesh=mesh,
        in_specs=(
            P(("groups", "fac"), None, None),
            P(("groups", "fac"), None, None),
            P(("groups", "fac"), None, None),
            P(("groups", "fac"), None, None),
            P("groups", None, "fac"),
        ),
        out_specs=(P(("groups", "fac"), None, None), P("groups", None, "fac")),
        check_vma=False,
    )
```

profile of v0, /device:TPU:3, one launch (start us, length us, event | category | flops | bytes accessed | tf_op | source)
XLA Modules:
  0.0 562.0 jit_solution(9362236796377634353)
XLA Ops:
  7.2 6.5 %all-to-all-start = ((f32[64,96,128]{2,1,0:T(8,128)}), f32[64,96,128]{2,1,0:T(8,128)}, u32[]{:S(2)}, u32[]{:S(2)}) async-start(f32[64,96,128]{2,1,0:T(8,128)} %param.34), calls=%async_computation | async-start | bytes 6291456 | tf_op jit(solution)/shard_map/all_to_all | solution.py:190
  13.8 3.3 copy.124
  17.1 5.8 %fusion.127 = f32[96,8192]{0,1:S(1)} fusion(f32[96,96]{1,0:T(8,128)S(1)} %copy-done.20, f32[96,8192]{0,1:T(8,128)} %bitcast.150), kind=kOutput, calls=%fused_computation.137 | convolution fusion | flops 905969664 | bytes 6328320
  22.9 3.6 fusion.126
  26.5 6.6 %fusion.37 = f32[2,96,64,64]{1,3,2,0:T(8,128)S(1)} fusion(f32[64,64,1,1]{0,1,3,2:T(8,128)S(1)} %copy-done.13, f32[2,96,64,64]{1,3,2,0:T(8,128)S(1)} %bitcast.154), kind=kOutput, calls=%fused_computation.56 | convolution fusion | flops 603979776 | bytes 6307840 | tf_op jit(solution)/shard_map/csba,bk->cska/dot_general | solution.py:28
  33.1 6.8 %fusion.35 = f32[2,96,64,64]{1,3,2,0:T(8,128)S(1)} fusion(f32[64,64,1,1]{0,1,3,2:T(8,128)S(1)} %copy-done.10, f32[2,96,64,64]{1,3,2,0:T(8,128)S(1)} %bitcast.155), kind=kOutput, calls=%fused_computation.54 | convolution fusion | flops 603979776 | bytes 6307840 | tf_op jit(solution)/shard_map/csba,bk->cska/dot_general | solution.py:28
  39.9 6.6 %fusion.60 = f32[2,96,64,64]{1,3,2,0:T(8,128)S(1)} fusion(f32[2,96,64,64]{1,3,2,0:T(8,128)S(1)} %fusion.37, f32[64,64,1,1]{0,1,3,2:T(8,128)S(1)} %copy-done.10, f32[2,96,64,64]{1,3,2,0:T(8,128)S(1)} %bitcast.152), kind=kOutput, calls=%fused_computation.80 | convolution fusion | flops 604766208 | bytes 9453568 | tf_op jit(solution)/shard_map/csba,bk->cska/dot_general | solution.py:28
  46.5 11.3 %fusion.13 = (f32[2,96,64,64]{1,2,3,0:T(8,128)}, f32[2,96,64,64]{1,2,3,0:T(8,128)S(1)}) fusion(f32[2,96,64,64]{1,3,2,0:T(8,128)S(1)} %fusion.60, f32[64,64]{0,1:T(8,128)S(1)} %copy-done.15, f32[64,64]{0,1:T(8,128)S(1)} %copy-done.9, f32[2,96,64,64]{1,3,2,0:T(8,128)S(1)} %fusion.35, f32[64,64,1,1]{0,1,3,2:T(8,128)S(1)} %copy-done.13, ...), kind=kOutput, calls=%fused_computation.20 | convolution fusion | flops 609484800 | bytes 15777792 | tf_op jit(solution)/shard_map/csba,bk->cska/dot_general | solution.py:28
  57.8 7.1 %fusion.29 = f32[2,96,64,64]{1,3,2,0:T(8,128)} fusion(f32[64,64,1,1]{0,1,3,2:T(8,128)S(1)} %copy-done.13, f32[2,96,64,64]{1,2,3,0:T(8,128)S(1)} %get-tuple-element.5), kind=kOutput, calls=%fused_computation.48 | convolution fusion | flops 603979776 | bytes 6307840 | tf_op jit(solution)/shard_map/cska,aj->csjk/dot_general | solution.py:28
  64.9 7.1 %fusion.27 = f32[2,96,64,64]{1,3,2,0:T(8,128)} fusion(f32[64,64,1,1]{0,1,3,2:T(8,128)S(1)} %copy-done.10, f32[2,96,64,64]{1,2,3,0:T(8,128)S(1)} %get-tuple-element.5), kind=kOutput, calls=%fused_computation.46 | convolution fusion | flops 603979776 | bytes 6307840 | tf_op jit(solution)/shard_map/cska,aj->csjk/dot_general | solution.py:28
  72.0 5.3 copy.132
  77.2 9.7 %subtract_bitcast_fusion.1 = f32[2,96,64,64]{1,2,3,0:T(8,128)S(1)} fusion(f32[2,96,64,64]{1,3,2,0:T(8,128)} %fusion.29, f32[64,64,1,1]{0,1,3,2:T(8,128)S(1)} %copy-done.10, f32[2,96,64,64]{1,2,3,0:T(8,128)} %get-tuple-element.4), kind=kOutput, calls=%fused_computation.37 | convolution fusion | flops 604766208 | bytes 9453568 | tf_op jit(solution)/shard_map/cska,aj->csjk/dot_general | solution.py:28
  86.9 4.4 copy.131
  91.3 5.1 copy.123
  96.4 5.3 copy.137
  101.8 9.7 %add_bitcast_fusion.1 = f32[2,96,64,64]{1,2,3,0:T(8,128)S(1)} fusion(f32[2,96,64,64]{1,3,2,0:T(8,128)} %fusion.27, f32[64,64,1,1]{0,1,3,2:T(8,128)S(1)} %copy-done.13, f32[2,96,64,64]{1,2,3,0:T(8,128)} %get-tuple-element.4), kind=kOutput, calls=%fused_computation.36 | convolution fusion | flops 604766208 | bytes 9453568 | tf_op jit(solution)/shard_map/cska,aj->csjk/dot_general | solution.py:28
  111.5 4.4 copy.136
  115.8 11.3 %fusion.12 = (f32[2,96,4096]{1,2,0:T(8,128)}, f32[2,96,4096]{1,2,0:T(8,128)}) fusion(f32[2,96,4096]{1,2,0:T(8,128)} %copy.132, f32[2,96,64,64]{1,3,2,0:T(8,128)} %copy.131, s32[2,96,4096]{1,2,0:T(8,128)} %copy.123, f32[2,96,4096]{1,2,0:T(8,128)} %copy.137, f32[2,96,64,64]{1,3,2,0:T(8,128)} %copy.136), kind=kLoop, calls=%fused_computation.17 | loop fusion | flops 3932160 | bytes 22020096 | tf_op jit(solution)/shard_map/mul | solution.py:85
  127.1 10.9 %fusion.19 = f32[2,96,64,64]{1,3,2,0:T(8,128)} fusion(f32[64,64,1,1]{0,1,3,2:T(8,128)S(1)} %copy-done.10, f32[2,96,64,64]{1,3,2,0:T(8,128)} %bitcast.164), kind=kOutput, calls=%fused_computation.38 | convolution fusion | flops 603979776 | bytes 6307840 | tf_op jit(solution)/shard_map/csjk,ja->cska/dot_general | solution.py:28
  138.0 7.1 %fusion.21 = f32[2,96,64,64]{1,3,2,0:T(8,128)} fusion(f32[64,64,1,1]{0,1,3,2:T(8,128)S(1)} %copy-done.12, f32[2,96,64,64]{1,3,2,0:T(8,128)S(1)} %bitcast.165), kind=kOutput, calls=%fused_computation.40 | convolution fusion | flops 603979776 | bytes 6307840 | tf_op jit(solution)/shard_map/csjk,ja->cska/dot_general | solution.py:28
  145.0 7.1 %fusion.23 = f32[2,96,64,64]{1,3,2,0:T(8,128)} fusion(f32[64,64,1,1]{0,1,3,2:T(8,128)S(1)} %copy-done.12, f32[2,96,64,64]{1,3,2,0:T(8,128)S(1)} %bitcast.162), kind=kOutput, calls=%fused_computation.42 | convolution fusion | flops 603979776 | bytes 6307840 | tf_op jit(solution)/shard_map/csjk,ja->cska/dot_general | solution.py:28
  152.2 7.2 %fusion.25 = f32[2,96,64,64]{1,3,2,0:T(8,128)} fusion(f32[64,64,1,1]{0,1,3,2:T(8,128)S(1)} %copy-done.10, f32[2,96,64,64]{1,3,2,0:T(8,128)S(1)} %bitcast.163), kind=kOutput, calls=%fused_computation.44 | convolution fusion | flops 603979776 | bytes 6307840 | tf_op jit(solution)/shard_map/csjk,ja->cska/dot_general | solution.py:28
  159.4 17.0 %copy_add_fusion = (f32[2,96,64,64]{1,2,3,0:T(8,128)S(1)}, f32[2,96,64,64]{1,2,3,0:T(8,128)}) fusion(f32[2,96,64,64]{1,3,2,0:T(8,128)} %fusion.19, f32[2,96,64,64]{1,3,2,0:T(8,128)} %fusion.23, f32[2,96,64,64]{1,3,2,0:T(8,128)} %fusion.21, f32[2,96,64,64]{1,3,2,0:T(8,128)} %fusion.25), kind=kLoop, calls=%fused_computation.29 | loop fusion | flops 1572864 | bytes 18874368 | tf_op jit(solution)/shard_map/add | solution.py:61
  176.4 6.7 %fusion.74 = f32[2,96,64,64]{1,3,2,0:T(8,128)S(1)} fusion(f32[64,64,1,1]{0,1,3,2:T(8,128)S(1)} %copy-done.12, f32[2,96,64,64]{1,2,3,0:T(8,128)S(1)} %get-tuple-element.26, f32[2,96,64,64]{1,2,3,0:T(8,128)} %get-tuple-element.27, f32[64,64]{0,1:T(8,128)S(1)} %copy-done.11, f32[64,64]{0,1:T(8,128)S(1)} %copy-done.9), kind=kOutput, calls=%fused_computation.85 | convolution fusion | flops 606339072 | bytes 9486336 | tf_op jit(solution)/shard_map/cska,kb->csba/dot_general | solution.py:28
  183.1 5.5 add_bitcast_fusion
  188.7 6.5 %fusion.15 = f32[2,64,64,96]{3,2,1,0:T(8,128)S(1)} fusion(f32[96,96,1,1]{1,0,3,2:T(8,128)S(1)} %copy-done.19, f32[2,96,64,64]{1,2,3,0:T(8,128)S(1)} %add_bitcast_fusion), kind=kOutput, calls=%fused_computation.25 | convolution fusion | flops 905969664 | bytes 6328320 | tf_op jit(solution)/shard_map/csba,sr->crba/dot_general | solution.py:28
  195.2 5.3 fusion.75
  200.6 5.3 subtract_bitcast_fusion
  205.9 7.4 %fusion.70 = f32[2,64,64,96]{3,2,1,0:T(8,128)} fusion(f32[2,64,64,96]{3,2,1,0:T(8,128)S(1)} %fusion.15, f32[96,96,1,1]{1,0,3,2:T(8,128)S(1)} %copy-done.18, f32[2,96,64,64]{1,2,3,0:T(8,128)S(1)} %subtract_bitcast_fusion), kind=kOutput, calls=%fused_computation.82 | convolution fusion | flops 906756096 | bytes 9474048 | tf_op jit(solution)/shard_map/csba,sr->crba/dot_general | solution.py:28
  213.3 5.3 copy.149
  218.6 5.2 copy.147
  223.8 1.9 slice.211
  225.7 0.9 copy-done.2
  226.6 0.1 fusion.121
  227.0 0.8 fusion.94
  227.9 1.5 fusion.76
  229.4 2.5 fusion.48
  232.0 2.6 pad_maximum_fusion
  234.6 7.8 %copy.148 = f32[2,96,32,134]{3,2,1,0:T(8,128)} copy(f32[2,96,32,134]{1,3,2,0:T(8,128)} %pad_maximum_fusion) | data formatting | bytes 6586368 | tf_op jit(solution)/shard_map/concatenate | solution.py:169
  242.4 8.3 %fusion.128 = f32[2,96,32,128]{3,2,1,0:T(8,128)} fusion(f32[2,96,32,134]{3,2,1,0:T(8,128)} %copy.148, f32[134,128,1,1]{1,0,3,2:T(8,128)S(1)} %copy-done.17), kind=kOutput, calls=%fused_computation.138 | convolution fusion | flops 1264582656 | bytes 6507520 | tf_op jit(solution)/shard_map/...m,mk->...k/dot_general | solution.py:28
  250.6 4.9 reshape.48
  255.6 6.3 %fusion.9 = f32[2,96,4096]{2,1,0:T(8,128)S(1)} fusion(f32[2,96,4096]{2,1,0:T(8,128)S(1)} %copy-done.6, f32[2,96,4096]{2,1,0:T(8,128)} %copy.149, f32[2,96,4096]{2,1,0:T(8,128)} %reshape.48, f32[96,96,1]{0,1,2:T(8,128)S(1)} %copy-done.14), kind=kOutput, calls=%fused_computation.10 | convolution fusion | flops 909115392 | bytes 12619776 | tf_op jit(solution)/shard_map/sr,csn->crn/dot_general | solution.py:28
  261.9 3.3 fusion.45
  265.3 0.5 copy.171
  265.9 0.1 slice.213
  266.0 0.4 slice.212
  266.4 0.4 copy-done.16
  266.7 5.5 fusion
  272.2 1.2 fusion.123
  273.5 0.4 slice.215
  273.9 1.1 maximum_maximum_fusion
  275.0 8.4 %fusion.43 = f32[2,96,32,64]{1,3,2,0:T(8,128)S(1)} fusion(f32[70,64,1,1]{0,1,3,2:T(8,128)S(1)} %copy-done.22, f32[2,96,32,70]{3,2,1,0:T(8,128)S(1)} %maximum_maximum_fusion), kind=kOutput, calls=%fused_computation.63 | convolution fusion | flops 330301440 | bytes 3311104 | tf_op jit(solution)/shard_map/...m,mk->...k/dot_general | solution.py:28
  283.4 1.2 fusion.124
  284.7 1.1 fusion.88
  285.8 1.1 fusion.125
  286.9 3.1 copy.170
  290.0 1.7 fusion.106
  291.7 7.0 %multiply_reduce_fusion = (f32[96,32,128]{0,2,1:T(8,128)}, f32[2,96,32,128]{1,3,2,0:T(8,128)}) fusion(f32[2,96,32,64]{1,3,2,0:T(8,128)} %copy.170, f32[2,96,32,32]{1,3,2,0:T(8,128)} %get-tuple-element.23, f32[2,96,32,16]{1,3,2,0:T(8,128)} %get-tuple-element.25, f32[2,96,32,16]{1,3,2,0:T(8,128)S(1)} %fusion.106, f32[32,2,96,128]{2,3,0,1:T(8,128)} %copy.147), kind=kLoop, calls=%fused_computation.31 | loop fusion | flops 5111808 | bytes 11010048 | tf_op jit(solution)/shard_map/reduce_sum | solution.py:202
  298.7 133.5 %all-reduce.2.cloned.1.call-done = f32[96,4096]{0,1:T(8,128)} async-done(((f32[96,4096]{0,1:T(8,128)}), f32[96,4096]{0,1:T(8,128)}) %all-reduce.2.cloned.1.call-update) | async-done | bytes 1572880 | tf_op jit(solution)/shard_map/psum | solution.py:202
  432.2 2.4 multiply_maximum_fusion
  434.6 0.5 copy-done.7
  435.0 15.1 %copy_divide_fusion = f32[2,96,4096]{1,0,2:T(2,128)S(1)} fusion(f32[2,96,4096]{1,2,0:T(8,128)S(1)} %bitcast.169, f32[96,4096]{0,1:T(8,128)S(1)} %multiply_maximum_fusion), kind=kLoop, calls=%fused_computation.24 | loop fusion | flops 786432 | bytes 7864320 | tf_op jit(solution)/shard_map/div | solution.py:203
  450.2 98.1 %all_to_all.33 = f32[2,96,4096]{1,0,2:T(2,128)} all-to-all(f32[2,96,4096]{1,0,2:T(2,128)S(1)} %copy_divide_fusion), channel_id=1, replica_groups=mesh['groups'=1,'fac'=32] {'fac'}, dimensions={2} | all-to-all | bytes 6291456 | tf_op jit(solution)/shard_map/all_to_all | solution.py:204
  548.3 6.6 %copy.154 = f32[32,2,96,128]{3,2,1,0:T(8,128)} copy(f32[32,2,96,128]{2,1,3,0:T(2,128)} %bitcast.171) | data formatting | bytes 6291456 | tf_op jit(solution)/shard_map/all_to_all | solution.py:204
  (71 shorter events, 0.7 us)
Async XLA Ops:
  7.2 6.6 %copy-start.5 = (f32[2,96,4096]{2,1,0:T(8,128)S(1)}, f32[2,96,4096]{2,1,0:T(8,128)}, u32[]{:S(2)}) copy-start(f32[2,96,4096]{2,1,0:T(8,128)} %param.30) | copy-start | bytes 9437188
  7.2 211.4 %all-to-all-start = ((f32[64,96,128]{2,1,0:T(8,128)}), f32[64,96,128]{2,1,0:T(8,128)}, u32[]{:S(2)}, u32[]{:S(2)}) async-start(f32[64,96,128]{2,1,0:T(8,128)} %param.34), calls=%async_computation | async-start | bytes 6291456 | tf_op jit(solution)/shard_map/all_to_all | solution.py:190
  13.7 3.4 copy-start.20
  13.7 418.5 %all-reduce.2.cloned.1.call-start = ((), (), s32[]{:S(2)}) async-start(), calls=%async_computation.2 | async-start | bytes 4194304 | tf_op jit(solution)/shard_map/psum | solution.py:202
  17.1 5.8 %copy-start.1 = (f32[2,96,4096]{1,2,0:T(8,128)S(1)}, f32[2,96,4096]{1,2,0:T(8,128)}, u32[]{:S(2)}) copy-start(f32[2,96,4096]{1,2,0:T(8,128)} %copy.124) | copy-start | bytes 9437188
  17.1 5.8 %copy-start.21 = (f32[96,96]{1,0:T(8,128)S(1)}, f32[96,96]{1,0:T(8,128)}, u32[]{:S(2)}) copy-start(f32[96,96]{1,0:T(8,128)} %constant.51.clone) | copy-start | bytes 110596
  22.9 3.6 copy-start.13
  26.5 6.6 %copy-start.10 = (f32[64,64,1,1]{0,1,3,2:T(8,128)S(1)}, f32[64,64,1,1]{0,1,3,2:T(8,128)}, u32[]{:S(2)}) copy-start(f32[64,64,1,1]{0,1,3,2:T(8,128)} %constant.72) | copy-start | bytes 49156
  39.9 6.6 %copy-start.9 = (f32[64,64]{0,1:T(8,128)S(1)}, f32[64,64]{0,1:T(8,128)}, u32[]{:S(2)}) copy-start(f32[64,64]{0,1:T(8,128)} %constant.55.clone) | copy-start | bytes 49156
  39.9 6.6 %copy-start.15 = (f32[64,64]{0,1:T(8,128)S(1)}, f32[64,64]{0,1:T(8,128)}, u32[]{:S(2)}) copy-start(f32[64,64]{0,1:T(8,128)} %constant.56.clone) | copy-start | bytes 49156
  127.1 10.9 %copy-start.4 = (f32[2,96,4096]{1,2,0:T(8,128)S(1)}, f32[2,96,4096]{1,2,0:T(8,128)}, u32[]{:S(2)}) copy-start(f32[2,96,4096]{1,2,0:T(8,128)} %get-tuple-element.19) | copy-start | bytes 9437188
  127.1 10.9 %copy-start.12 = (f32[64,64,1,1]{0,1,3,2:T(8,128)S(1)}, f32[64,64,1,1]{0,1,3,2:T(8,128)}, u32[]{:S(2)}) copy-start(f32[64,64,1,1]{0,1,3,2:T(8,128)} %constant.74) | copy-start | bytes 49156
  138.0 7.1 %copy-start.3 = (f32[2,96,4096]{1,2,0:T(8,128)S(1)}, f32[2,96,4096]{1,2,0:T(8,128)}, u32[]{:S(2)}) copy-start(f32[2,96,4096]{1,2,0:T(8,128)} %get-tuple-element.18) | copy-start | bytes 9437188
  159.4 17.0 %copy-start.11 = (f32[64,64]{0,1:T(8,128)S(1)}, f32[64,64]{0,1:T(8,128)}, u32[]{:S(2)}) copy-start(f32[64,64]{0,1:T(8,128)} %constant.58.clone) | copy-start | bytes 49156
  176.4 6.7 %copy-start = (f32[2,96,64,64]{1,2,3,0:T(8,128)S(1)}, f32[2,96,64,64]{1,2,3,0:T(8,128)}, u32[]{:S(2)}) copy-start(f32[2,96,64,64]{1,2,3,0:T(8,128)} %get-tuple-element.27) | copy-start | bytes 9437188
  183.1 5.6 copy-start.19
  200.5 5.4 copy-start.18
  223.8 2.8 copy-start.2
  223.8 3.2 copy-start.27
  226.6 1.3 copy-start.26
  226.8 2.6 copy-start.25
  234.6 7.8 %copy-start.17 = (f32[134,128,1,1]{1,0,3,2:T(8,128)S(1)}, f32[134,128,1,1]{1,0,3,2:T(8,128)}, u32[]{:S(2)}) copy-start(f32[134,128,1,1]{1,0,3,2:T(8,128)} %constant.80) | copy-start | bytes 205828
  250.6 4.9 copy-start.6
  250.6 5.0 copy-start.14
  261.9 3.4 copy-start.8
  265.8 0.9 copy-start.16
  273.9 1.1 copy-start.22
  275.0 9.6 %copy-start.23 = (f32[38,32,1,1]{0,1,3,2:T(8,128)S(1)}, f32[38,32,1,1]{0,1,3,2:T(8,128)}, u32[]{:S(2)}) copy-start(f32[38,32,1,1]{0,1,3,2:T(8,128)} %constant.84) | copy-start | bytes 14596
  285.8 4.2 copy-start.24
  432.2 2.8 copy-start.7
Sparse Core Ops, SparseCore 0:
  298.8 133.3 all-reduce.1
where the time goes:
time: 567 us; the launch traced here: 562 us
  matrix products  183 us (32%)
  waiting for transfers between devices  134 us (24%)
  blocking collectives  98.1 us (17%)
  local copies, waits for them, and re-layouts  69.9 us (12%)
  other arithmetic  56.4 us (10%)
  between operations  14.9 us (3%)
  starting transfers between devices  6.54 us (1%)
    dot_general x28, matrix products, contract(): jnp.einsum(pattern, left_side, right_side, precision=precise, preferred_e...  173 us
    psum x1, waiting for transfers between devices, shards(): summed = lax.psum(jnp.sum(lifted * lifted, axis=0), 'fac')  134 us
    all_to_all x1, blocking collectives, shards(): lax.all_to_all(shrunk, 'fac', split_axis=2, concat_axis=0, tiled=True)  98.1 us
    unnamed x62, local copies, waits for them, and re-layouts  24.6 us
    add x1, other arithmetic, complex_step(): contract(pattern, real_part, matrix[1])  17 us
    div x1, other arithmetic, shards(): shrunk = lifted / jnp.maximum(1.0, jnp.sqrt(summed) / ball_radius)  15.1 us
  transfers between devices with their start and end apart: 2, of which 1 were waited for; matrix products, arithmetic and copies ran while one was open for 36% of the time, Pallas kernels for 0%

commit v1 on v0

v1 whole, which is shorter than its diff:
```python
import jax
import jax.numpy as jnp
import ml_dtypes
import numpy as np
from jax import lax
from jax.experimental import pallas as pl
from jax.experimental.pallas import tpu as pltpu
from jax.sharding import PartitionSpec as P

LEVELS = 4
LANES = 128


low_pass = (
    0.2303778133088964,
    0.7148465705529155,
    0.6308807679298587,
    -0.0279837694168599,
    -0.1870348117190931,
    0.0308413818355607,
    0.0328830116668852,
    -0.010597401785069,
)
high_pass = tuple(((-1) ** tap_index * low_pass[7 - tap_index] for tap_index in range(8)))
primal_step = 0.6
dual_step = 0.8
ball_radius = 12.0
vmem_limit = 48 * 1024 * 1024


def split_table(matrix):
    high = np.asarray(matrix, np.float32).astype(ml_dtypes.bfloat16)
    low = (matrix - high.astype(np.float64)).astype(np.float32).astype(ml_dtypes.bfloat16)
    return [jnp.asarray(high), jnp.asarray(low)]


def halves(values):
    high = values.astype(jnp.bfloat16)
    return high, (values - high.astype(jnp.float32)).astype(jnp.bfloat16)


def dot(left, right):
    return jnp.dot(left, right, preferred_element_type=jnp.float32)


def times_table(values, high_ref, low_ref):
    high, low = halves(values)
    return dot(high, high_ref[...]) + (dot(low, high_ref[...]) + dot(high, low_ref[...]))


def table_times(high_ref, low_ref, values):
    high, low = halves(values)
    return dot(high_ref[...], high) + (dot(high_ref[...], low) + dot(low_ref[...], high))


def dft_angles(length):
    grid = np.arange(length)
    return 2.0 * np.pi * (np.outer(grid, grid) % length) / length


def row_tables(rows):
    angles = dft_angles(rows)
    cosine, sine = np.cos(angles) / np.sqrt(rows), np.sin(angles) / np.sqrt(rows)
    return np.concatenate([cosine, -sine], 0), np.concatenate([cosine, -sine], 1)


def lane_tables(tiles):
    lanes = np.arange(LANES)
    point = (LANES // tiles) * (lanes % tiles) + lanes // tiles
    angles = dft_angles(LANES)[point] / 1.0
    scale = 1.0 / np.sqrt(LANES * tiles)
    cosine, sine = np.cos(angles) * scale, np.sin(angles) * scale
    forward = np.block([[cosine, -sine], [sine, cosine]])
    backward = np.block([[cosine.T, sine.T], [-sine.T, cosine.T]])
    return forward, backward


def twist_table(tiles):
    angles = 2.0 * np.pi * np.outer(np.arange(tiles), np.arange(LANES)) / (tiles * LANES)
    both = np.concatenate([np.cos(angles), np.sin(angles)], 1)
    return jnp.asarray(np.repeat(both[:, None, :], 8, 1), jnp.float32)


def transform(points, sign):
    count = len(points)
    if count == 1:
        return points
    even = transform(points[0::2], sign)
    odd = transform(points[1::2], sign)
    half = count // 2
    first, second = [], []
    for index in range(half):
        real, imag = odd[index]
        if index == 0:
            pass
        elif 4 * index == count:
            real, imag = (-sign * imag, sign * real) if sign > 0 else (imag, -real)
        elif 8 * index == count:
            root = float(np.sqrt(0.5))
            real, imag = (
                ((real - imag) * root, (imag + real) * root)
                if sign > 0
                else ((real + imag) * root, (imag - real) * root)
            )
        elif 8 * index == 3 * count:
            root = float(np.sqrt(0.5))
            real, imag = (
                ((-real - imag) * root, (real - imag) * root)
                if sign > 0
                else ((imag - real) * root, (-real - imag) * root)
            )
        else:
            cosine = float(np.cos(2.0 * np.pi * index / count))
            sine = float(sign * np.sin(2.0 * np.pi * index / count))
            real, imag = real * cosine - imag * sine, real * sine + imag * cosine
        first.append((even[index][0] + real, even[index][1] + imag))
        second.append((even[index][0] - real, even[index][1] - imag))
    return first + second


def turn(slabs):
    slabs = list(slabs)
    lane = lax.broadcasted_iota(jnp.int32, slabs[0].shape, 1)
    step = 1
    while step < len(slabs):
        marked = (lane & step) != 0
        for low in range(len(slabs)):
            if low & step:
                continue
            one, other = slabs[low], slabs[low + step]
            slabs[low] = jnp.where(marked, pltpu.roll(other, step, 1), one)
            slabs[low + step] = jnp.where(marked, other, pltpu.roll(one, LANES - step, 1))
        step *= 2
    return slabs


def gradient_kernel(
    sky, meas_re, meas_im, mask, row_fh, row_fl, row_bh, row_bl,
    lane_fh, lane_fl, lane_bh, lane_bl, twist, out, field, real_field,
):
    tiles, rows, _ = real_field.shape
    group = 4

    def tile(index):
        return pl.ds(index * LANES, LANES)

    def turn_in(step, carry):
        here = pl.ds(pl.multiple_of(step * 8, 8), 8)
        for index, slab in enumerate(turn([sky[0, here, tile(t)] for t in range(tiles)])):
            real_field[index, here, :] = slab
        return carry

    lax.fori_loop(0, rows // 8, turn_in, 0)

    def forward(step, carry):
        slabs = [real_field[step * group + i] for i in range(group)]
        both = table_times(row_fh, row_fl, jnp.concatenate(slabs, 1))
        parts = [
            jnp.concatenate([both[:rows, i * LANES : (i + 1) * LANES], both[rows:, i * LANES : (i + 1) * LANES]], 1)
            for i in range(group)
        ]
        result = times_table(jnp.concatenate(parts, 0), lane_fh, lane_fl)
        for i in range(group):
            field[step * group + i] = result[i * rows : (i + 1) * rows]
        return carry

    lax.fori_loop(0, tiles // group, forward, 0)

    def middle(step, carry):
        here = pl.ds(pl.multiple_of(step * 8, 8), 8)
        points = []
        for t in range(tiles):
            real, imag = field[t, here, :LANES], field[t, here, LANES:]
            cosine, sine = twist[t, :, :LANES], twist[t, :, LANES:]
            points.append((real * cosine + imag * sine, imag * cosine - real * sine))
        spectrum = transform(points, -1.0)
        misfit = []
        for t in range(tiles):
            weight = mask[0, here, tile(t)].astype(jnp.float32)
            misfit.append(
                (
                    weight * (spectrum[t][0] - meas_re[0, here, tile(t)]),
                    weight * (spectrum[t][1] - meas_im[0, here, tile(t)]),
                )
            )
        for t, (real, imag) in enumerate(transform(misfit, 1.0)):
            cosine, sine = twist[t, :, :LANES], twist[t, :, LANES:]
            field[t, here, :LANES] = real * cosine - imag * sine
            field[t, here, LANES:] = real * sine + imag * cosine
        return carry

    lax.fori_loop(0, rows // 8, middle, 0)

    def backward(step, carry):
        parts = jnp.concatenate([field[step * group + i] for i in range(group)], 0)
        result = times_table(parts, lane_bh, lane_bl)
        real = [result[i * rows : (i + 1) * rows, :LANES] for i in range(group)]
        imag = [result[i * rows : (i + 1) * rows, LANES:] for i in range(group)]
        both = jnp.concatenate([jnp.concatenate(real, 1), jnp.concatenate(imag, 1)], 0)
        result = table_times(row_bh, row_bl, both)
        for i in range(group):
            real_field[step * group + i] = result[:, i * LANES : (i + 1) * LANES]
        return carry

    lax.fori_loop(0, tiles // group, backward, 0)

    def turn_out(step, carry):
        here = pl.ds(pl.multiple_of(step * 8, 8), 8)
        for index, slab in enumerate(turn([real_field[t, here, :] for t in range(tiles)])):
            out[0, here, tile(index)] = slab
        return carry

    lax.fori_loop(0, rows // 8, turn_out, 0)


def whole(array):
    return pl.BlockSpec(array.shape, lambda c: (0,) * array.ndim)


def channel_block(rows, columns):
    return pl.BlockSpec((1, rows, columns), lambda c: (c, 0, 0))


def data_gradient(sky_image, measured_real, measured_imaginary, sampling_mask):
    channels, rows, columns = sky_image.shape
    tiles = columns // LANES
    row_forward, row_backward = row_tables(rows)
    lane_forward, lane_backward = lane_tables(tiles)
    tables = (
        split_table(row_forward)
        + split_table(row_backward)
        + split_table(lane_forward)
        + split_table(lane_backward)
        + [twist_table(tiles)]
    )
    block = channel_block(rows, columns)
    return pl.pallas_call(
        gradient_kernel,
        name="gradient",
        grid=(channels,),
        in_specs=[block] * 4 + [whole(table) for table in tables],
        out_specs=block,
        out_shape=jax.ShapeDtypeStruct(sky_image.shape, jnp.float32),
        scratch_shapes=[
            pltpu.VMEM((tiles, rows, 2 * LANES), jnp.float32),
            pltpu.VMEM((tiles, rows, LANES), jnp.float32),
        ],
        compiler_params=pltpu.CompilerParams(vmem_limit_bytes=vmem_limit),
        cost_estimate=pl.CostEstimate(
            flops=3 * 2 * channels * rows * columns * 1400, bytes_accessed=20 * channels * rows * columns, transcendentals=0
        ),
    )(sky_image, measured_real, measured_imaginary, sampling_mask, *tables)


def row_matrix(length):
    current = np.eye(length)
    details = []
    for level_index in range(LEVELS):
        width_now = current.shape[0]
        half_size = width_now // 2
        lower = np.zeros((half_size, width_now))
        upper = np.zeros((half_size, width_now))
        for target in range(half_size):
            for tap_index in range(8):
                lower[target, (2 * target + tap_index) % width_now] += low_pass[tap_index]
                upper[target, (2 * target + tap_index) % width_now] += high_pass[tap_index]
        details.insert(0, upper @ current)
        current = lower @ current
    return np.concatenate([current] + details, 0)


def facet_matrix(width):
    long = 4 * width
    full = row_matrix(long)
    picked = []
    start, size = 0, width >> LEVELS
    for level_index in range(LEVELS + 1):
        picked.append(full[start : start + size])
        start = (long >> LEVELS) << level_index
        size = (width >> LEVELS) << level_index
    block = np.concatenate(picked, 0)
    assert np.all(block[:, 2 * width :] == 0.0)
    return block[:, : 2 * width].T


def wavelet_kernel(
    sky, gradient, coefficients, row_sh, row_sl, row_ah, row_al, col_sh, col_sl, col_ah, col_al,
    next_image, analysed, turned,
):
    facets, _, rows, width = coefficients.shape
    group = 4

    def primal(step, carry):
        parts = []
        for i in range(group):
            index = step * group + i
            parts.append(
                jnp.concatenate([coefficients[index, 0], coefficients[(index + facets - 1) % facets, 0]], 1)
            )
        prior = times_table(jnp.concatenate(parts, 0), col_sh, col_sl)
        prior = jnp.concatenate([prior[i * rows : (i + 1) * rows] for i in range(group)], 1)
        prior = table_times(row_sh, row_sl, prior)
        here = pl.ds(pl.multiple_of(step * (group * width), group * width), group * width)
        old = sky[0, :, here]
        new = jnp.maximum(old - primal_step * (gradient[0, :, here] + prior), 0.0)
        next_image[0, :, here] = new
        result = table_times(row_ah, row_al, 2.0 * new - old)
        for i in range(group):
            turned[step * group + i] = result[:, i * width : (i + 1) * width]
        return carry

    lax.fori_loop(0, facets // group, primal, 0)

    def columns(step, carry):
        parts = []
        for i in range(group):
            index = step * group + i
            parts.append(jnp.concatenate([turned[index], turned[(index + 1) % facets]], 1))
        result = times_table(jnp.concatenate(parts, 0), col_ah, col_al)
        for i in range(group):
            analysed[step * group + i, 0] = result[i * rows : (i + 1) * rows]
        return carry

    lax.fori_loop(0, facets // group, columns, 0)


def primal_step_and_analysis(sky_image, gradient, coefficients):
    channels, rows, columns = sky_image.shape
    facets, width = coefficients.shape[0], coefficients.shape[3]
    row_analysis = row_matrix(rows)
    col_analysis = facet_matrix(width)
    col_synthesis = np.concatenate([col_analysis[:width].T, col_analysis[width:].T], 0)
    tables = (
        split_table(row_analysis.T)
        + split_table(row_analysis)
        + split_table(col_synthesis)
        + split_table(col_analysis)
    )
    block = channel_block(rows, columns)
    facet_block = pl.BlockSpec((facets, 1, rows, width), lambda c: (0, c, 0, 0))
    return pl.pallas_call(
        wavelet_kernel,
        name="wavelet",
        grid=(channels,),
        in_specs=[block, block, facet_block] + [whole(table) for table in tables],
        out_specs=[block, facet_block],
        out_shape=[
            jax.ShapeDtypeStruct(sky_image.shape, jnp.float32),
            jax.ShapeDtypeStruct(coefficients.shape, jnp.float32),
        ],
        scratch_shapes=[pltpu.VMEM((facets, rows, width), jnp.float32)],
        compiler_params=pltpu.CompilerParams(vmem_limit_bytes=vmem_limit),
        cost_estimate=pl.CostEstimate(
            flops=3 * 2 * channels * rows * columns * 700, bytes_accessed=20 * channels * rows * columns, transcendentals=0
        ),
    )(sky_image, gradient, coefficients, *tables)


def shrink_kernel(dual, update, out):
    total = jnp.zeros(dual.shape[1:], jnp.float32)
    for channel in range(dual.shape[0]):
        lifted = dual[channel] + dual_step * update[channel]
        out[channel] = lifted
        total = total + lifted * lifted
    factor = 1.0 / jnp.maximum(1.0, jnp.sqrt(total) / ball_radius)
    for channel in range(dual.shape[0]):
        out[channel] = out[channel] * factor


def shrink(dual, update):
    channels, rows, width = dual.shape
    block = pl.BlockSpec((channels, 8, width), lambda r: (0, r, 0))
    return pl.pallas_call(
        shrink_kernel,
        name="shrink",
        grid=(rows // 8,),
        in_specs=[block, block],
        out_specs=block,
        out_shape=jax.ShapeDtypeStruct(dual.shape, jnp.float32),
        compiler_params=pltpu.CompilerParams(vmem_limit_bytes=vmem_limit),
        cost_estimate=pl.CostEstimate(flops=5 * dual.size, bytes_accessed=12 * dual.size, transcendentals=0),
    )(dual, update)


def shards(sky_image, measured_real, measured_imaginary, sampling_mask, dual_field):
    channels, rows, columns = sky_image.shape
    facets = lax.axis_size("fac")
    local_dual = lax.all_to_all(dual_field, "fac", split_axis=0, concat_axis=0, tiled=True)
    gradient = data_gradient(sky_image, measured_real, measured_imaginary, sampling_mask)
    next_image, analysed = primal_step_and_analysis(
        sky_image, gradient, local_dual.reshape(facets, channels, rows, columns // facets)
    )
    update = lax.all_to_all(
        analysed.reshape(dual_field.shape), "fac", split_axis=0, concat_axis=0, tiled=True
    )
    return (next_image, shrink(dual_field, update))


def solution(mesh):
    return jax.shard_map(
        shards,
        mesh=mesh,
        in_specs=(
            P(("groups", "fac"), None, None),
            P(("groups", "fac"), None, None),
            P(("groups", "fac"), None, None),
            P(("groups", "fac"), None, None),
            P("groups", None, "fac"),
        ),
        out_specs=(P(("groups", "fac"), None, None), P("groups", None, "fac")),
        check_vma=False,
    )
```

time: 567 us -> 188 us (0.33)
  matrix products: 183 us -> 0 us
  waiting for transfers between devices: 134 us -> 20 us
  Pallas kernels: 0 us -> 81.1 us
  local copies, waits for them, and re-layouts: 69.9 us -> 1.78 us
  other arithmetic: 56.4 us -> 0 us
  blocking collectives: 98.1 us -> 75.4 us
  between operations: 14.9 us -> 0.9 us
    dot_general x28 -> x0, matrix products: 173 us -> none  [contract(): jnp.einsum(pattern, left_side, right_side, precision=precise, preferred_e...]
    psum x1 -> x0, waiting for transfers between devices: 134 us -> none  [shards(): summed = lax.psum(jnp.sum(lifted * lifted, axis=0), 'fac')]
    pallas_call x0 -> x3, Pallas kernels: none -> 81.1 us  [the longest x1 48.6 us: data_gradient(): pl.pallas_call(gradient_kernel, name='gradient', grid=(channels,), in_spe...]
    unnamed x62 -> x38, local copies, waits for them, and re-layouts: 24.6 us -> 1.78 us
    all_to_all x1, blocking collectives: 98.1 us -> 75.4 us  [shards(): lax.all_to_all(analysed.reshape(dual_field.shape), 'fac', split_axis=0, c...]
    all_to_all x1, waiting for transfers between devices: 0.01 us -> 20 us  [shards(): lax.all_to_all(dual_field, 'fac', split_axis=0, concat_axis=0, tiled=True)]
    add x1 -> x0, other arithmetic: 17 us -> none  [complex_step(): contract(pattern, real_part, matrix[1])]
    div x1 -> x0, other arithmetic: 15.1 us -> none  [shards(): shrunk = lifted / jnp.maximum(1.0, jnp.sqrt(summed) / ball_radius)]
  transfers between devices with their start and end apart: 2 -> 1, of which waited for: 1 -> 1; matrix products, arithmetic and copies ran while one was open for 36% -> 0% of each run, Pallas kernels for 0% -> 26%
where the time goes in v1:
time: 188 us; the launch traced here: 186 us
  Pallas kernels  81.1 us (43%)
  blocking collectives  75.4 us (40%)
  waiting for transfers between devices  20 us (11%)
  starting transfers between devices  6.49 us (3%)
    all_to_all x1, blocking collectives, shards(): lax.all_to_all(analysed.reshape(dual_field.shape), 'fac', split_axis=0, c...  75.4 us
    pallas_call x1, Pallas kernels, data_gradient(): pl.pallas_call(gradient_kernel, name='gradient', grid=(channels,), in_spe...  48.6 us
    pallas_call x1, Pallas kernels, primal_step_and_analysis(): pl.pallas_call(wavelet_kernel, name='wavelet', grid=(channels,), in_specs...  24 us
    all_to_all x1, waiting for transfers between devices, shards(): lax.all_to_all(dual_field, 'fac', split_axis=0, concat_axis=0, tiled=True)  20 us
    pallas_call x1, Pallas kernels, shrink(): pl.pallas_call(shrink_kernel, name='shrink', grid=(rows // 8,), in_specs=...  8.42 us
    all_to_all x1, starting transfers between devices, shards(): lax.all_to_all(dual_field, 'fac', split_axis=0, concat_axis=0, tiled=True)  6.49 us
  transfers between devices with their start and end apart: 1, of which 1 were waited for; matrix products, arithmetic and copies ran while one was open for 0% of the time, Pallas kernels for 26%

profile of v1, /device:TPU:3, one launch (start us, length us, event | category | flops | bytes accessed | tf_op | source)
XLA Modules:
  0.0 185.7 jit_solution(10181904007243140735)
XLA Ops:
  0.6 0.0 copy-start.1
  0.6 0.0 copy-start.2
  0.7 0.0 copy-start.3
  0.7 0.0 copy-start.4
  0.7 0.0 copy-start.5
  0.7 0.0 copy-start.10
  0.7 0.0 copy-start.11
  0.7 0.0 copy-start.12
  0.7 0.0 copy-start.13
  0.7 6.5 %all-to-all-start = ((f32[64,96,128]{2,1,0:T(8,128)}), f32[64,96,128]{2,1,0:T(8,128)}, u32[]{:S(2)}, u32[]{:S(2)}) async-start(f32[64,96,128]{2,1,0:T(8,128)} %dual.1), calls=%async_computation | async-start | bytes 6291456 | tf_op jit(solution)/shard_map/all_to_all | solution.py:388
  7.2 0.0 copy-done.1
  7.3 0.0 copy-done.2
  7.3 0.0 copy-done.3
  7.3 0.0 copy-done.4
  7.3 0.0 copy-done.5
  7.3 0.0 copy-done.10
  7.3 0.0 copy-done.11
  7.3 0.0 copy-done.12
  7.3 0.0 copy-done.13
  7.3 0.0 copy-start.6
  7.3 0.0 copy-start.7
  7.4 0.0 copy-start.8
  7.4 0.0 copy-start.9
  7.4 0.0 copy-start.14
  7.4 0.0 copy-start.15
  7.4 0.0 copy-start.16
  7.4 0.0 copy-start.17
  7.4 48.6 %gradient.1 = f32[2,96,4096]{2,1,0:T(8,128)S(1)} custom-call(f32[2,96,4096]{2,1,0:T(8,128)} %sky.3, f32[2,96,4096]{2,1,0:T(8,128)} %meas_re.1, f32[2,96,4096]{2,1,0:T(8,128)} %meas_im.1, s32[2,96,4096]{2,1,0:T(8,128)} %mask.1, bf16[192,96]{1,0:T(8,128)(2,1)S(1)} %copy-done.13, bf16[192,96]{1,0:T(8,128)(2,1)S(1)} %copy-done.12, ...), custom_call_target="tpu_custom_call" | custom-call | flops 6606028800 | bytes 15728640 | tf_op jit(solution)/shard_map/gradient/pallas_call | solution.py:237
  56.0 0.0 copy-start.18
  56.0 1.7 copy-done.18
  57.7 20.0 %all-to-all-done = f32[64,96,128]{2,1,0:T(8,128)} async-done(((f32[64,96,128]{2,1,0:T(8,128)}), f32[64,96,128]{2,1,0:T(8,128)}, u32[]{:S(2)}, u32[]{:S(2)}) %all-to-all-start) | async-done | bytes 3145760 | tf_op jit(solution)/shard_map/all_to_all | solution.py:388
  77.7 0.0 copy-done.6
  77.7 0.0 copy-done.7
  77.7 0.0 copy-done.8
  77.7 0.0 copy-done.9
  77.7 0.0 copy-done.14
  77.7 0.0 copy-done.15
  77.8 0.0 copy-done.16
  77.8 0.0 copy-done.17
  77.8 24.0 %wavelet.1 = (f32[2,96,4096]{2,1,0:T(8,128)}, f32[32,2,96,128]{3,2,1,0:T(8,128)S(1)}) custom-call(f32[2,96,4096]{2,1,0:T(8,128)} %sky.3, f32[2,96,4096]{2,1,0:T(8,128)} %copy-done.18, f32[32,2,96,128]{3,2,1,0:T(8,128)} %bitcast.coefficients, bf16[96,96]{1,0:T(8,128)(2,1)S(1)} %copy-done.17, bf16[96,96]{1,0:T(8,128)(2,1)S(1)} %copy-done.16, ...), custom_call_target="tpu_custom_call" | custom-call | flops 3303014400 | bytes 15728640 | tf_op jit(solution)/shard_map/wavelet/pallas_call | solution.py:341
  101.8 0.0 copy-start
  101.8 75.4 %all_to_all.10.update = f32[64,96,128]{2,1,0:T(8,128)} all-to-all(f32[64,96,128]{2,1,0:T(8,128)S(1)} %bitcast.2), channel_id=1, replica_groups=mesh['groups'=1,'fac'=32] {'fac'}, dimensions={0} | all-to-all | bytes 6291456 | tf_op jit(solution)/shard_map/all_to_all | solution.py:393
  177.2 0.0 copy-done
  177.2 8.4 %shrink.1 = f32[64,96,128]{2,1,0:T(8,128)} custom-call(f32[64,96,128]{2,1,0:T(8,128)S(1)} %copy-done, f32[64,96,128]{2,1,0:T(8,128)} %all_to_all.10.update), custom_call_target="tpu_custom_call" | custom-call | flops 3932160 | bytes 9437184 | tf_op jit(solution)/shard_map/shrink/pallas_call | solution.py:373
Async XLA Ops:
  0.6 6.6 %copy-start.1 = (f32[32,8,256]{2,1,0:T(8,128)S(1)}, f32[32,8,256]{2,1,0:T(8,128)}, u32[]{:S(2)}) copy-start(f32[32,8,256]{2,1,0:T(8,128)} %constant.42.clone.twist) | copy-start | bytes 786436
  0.6 6.6 %copy-start.2 = (bf16[256,256]{1,0:T(8,128)(2,1)S(1)}, bf16[256,256]{1,0:T(8,128)(2,1)}, u32[]{:S(2)}) copy-start(bf16[256,256]{1,0:T(8,128)(2,1)} %constant.41.clone.lane_bl) | copy-start | bytes 393220
  0.7 6.6 %copy-start.3 = (bf16[256,256]{1,0:T(8,128)(2,1)S(1)}, bf16[256,256]{1,0:T(8,128)(2,1)}, u32[]{:S(2)}) copy-start(bf16[256,256]{1,0:T(8,128)(2,1)} %constant.40.clone.lane_bh) | copy-start | bytes 393220
  0.7 6.6 %copy-start.4 = (bf16[256,256]{1,0:T(8,128)(2,1)S(1)}, bf16[256,256]{1,0:T(8,128)(2,1)}, u32[]{:S(2)}) copy-start(bf16[256,256]{1,0:T(8,128)(2,1)} %constant.39.clone.lane_fl) | copy-start | bytes 393220
  0.7 6.6 %copy-start.5 = (bf16[256,256]{1,0:T(8,128)(2,1)S(1)}, bf16[256,256]{1,0:T(8,128)(2,1)}, u32[]{:S(2)}) copy-start(bf16[256,256]{1,0:T(8,128)(2,1)} %constant.38.clone.lane_fh) | copy-start | bytes 393220
  0.7 6.6 %copy-start.10 = (bf16[96,192]{1,0:T(8,128)(2,1)S(1)}, bf16[96,192]{1,0:T(8,128)(2,1)}, u32[]{:S(2)}) copy-start(bf16[96,192]{1,0:T(8,128)(2,1)} %constant.37.clone.row_bl) | copy-start | bytes 110596
  0.7 6.6 %copy-start.11 = (bf16[96,192]{1,0:T(8,128)(2,1)S(1)}, bf16[96,192]{1,0:T(8,128)(2,1)}, u32[]{:S(2)}) copy-start(bf16[96,192]{1,0:T(8,128)(2,1)} %constant.36.clone.row_bh) | copy-start | bytes 110596
  0.7 6.6 %copy-start.12 = (bf16[192,96]{1,0:T(8,128)(2,1)S(1)}, bf16[192,96]{1,0:T(8,128)(2,1)}, u32[]{:S(2)}) copy-start(bf16[192,96]{1,0:T(8,128)(2,1)} %constant.35.clone.row_fl) | copy-start | bytes 110596
  0.7 6.6 %copy-start.13 = (bf16[192,96]{1,0:T(8,128)(2,1)S(1)}, bf16[192,96]{1,0:T(8,128)(2,1)}, u32[]{:S(2)}) copy-start(bf16[192,96]{1,0:T(8,128)(2,1)} %constant.34.clone.row_fh) | copy-start | bytes 110596
  0.7 77.0 %all-to-all-start = ((f32[64,96,128]{2,1,0:T(8,128)}), f32[64,96,128]{2,1,0:T(8,128)}, u32[]{:S(2)}, u32[]{:S(2)}) async-start(f32[64,96,128]{2,1,0:T(8,128)} %dual.1), calls=%async_computation | async-start | bytes 6291456 | tf_op jit(solution)/shard_map/all_to_all | solution.py:388
  7.3 70.4 %copy-start.6 = (bf16[256,128]{1,0:T(8,128)(2,1)S(1)}, bf16[256,128]{1,0:T(8,128)(2,1)}, u32[]{:S(2)}) copy-start(bf16[256,128]{1,0:T(8,128)(2,1)} %constant.50.clone.col_al) | copy-start | bytes 196612
  7.3 70.4 %copy-start.7 = (bf16[256,128]{1,0:T(8,128)(2,1)S(1)}, bf16[256,128]{1,0:T(8,128)(2,1)}, u32[]{:S(2)}) copy-start(bf16[256,128]{1,0:T(8,128)(2,1)} %constant.49.clone.col_ah) | copy-start | bytes 196612
  7.4 70.4 %copy-start.8 = (bf16[256,128]{1,0:T(8,128)(2,1)S(1)}, bf16[256,128]{1,0:T(8,128)(2,1)}, u32[]{:S(2)}) copy-start(bf16[256,128]{1,0:T(8,128)(2,1)} %constant.48.clone.col_sl) | copy-start | bytes 196612
  7.4 70.4 %copy-start.9 = (bf16[256,128]{1,0:T(8,128)(2,1)S(1)}, bf16[256,128]{1,0:T(8,128)(2,1)}, u32[]{:S(2)}) copy-start(bf16[256,128]{1,0:T(8,128)(2,1)} %constant.47.clone.col_sh) | copy-start | bytes 196612
  7.4 70.4 %copy-start.14 = (bf16[96,96]{1,0:T(8,128)(2,1)S(1)}, bf16[96,96]{1,0:T(8,128)(2,1)}, u32[]{:S(2)}) copy-start(bf16[96,96]{1,0:T(8,128)(2,1)} %constant.46.clone.row_al) | copy-start | bytes 55300
  7.4 70.3 %copy-start.15 = (bf16[96,96]{1,0:T(8,128)(2,1)S(1)}, bf16[96,96]{1,0:T(8,128)(2,1)}, u32[]{:S(2)}) copy-start(bf16[96,96]{1,0:T(8,128)(2,1)} %constant.45.clone.row_ah) | copy-start | bytes 55300
  7.4 70.3 %copy-start.16 = (bf16[96,96]{1,0:T(8,128)(2,1)S(1)}, bf16[96,96]{1,0:T(8,128)(2,1)}, u32[]{:S(2)}) copy-start(bf16[96,96]{1,0:T(8,128)(2,1)} %constant.44.clone.row_sl) | copy-start | bytes 55300
  7.4 70.3 %copy-start.17 = (bf16[96,96]{1,0:T(8,128)(2,1)S(1)}, bf16[96,96]{1,0:T(8,128)(2,1)}, u32[]{:S(2)}) copy-start(bf16[96,96]{1,0:T(8,128)(2,1)} %constant.43.clone.row_sh) | copy-start | bytes 55300
  56.0 1.7 copy-start.18
  101.8 75.4 %copy-start = (f32[64,96,128]{2,1,0:T(8,128)S(1)}, f32[64,96,128]{2,1,0:T(8,128)}, u32[]{:S(2)}) copy-start(f32[64,96,128]{2,1,0:T(8,128)} %dual.1) | copy-start | bytes 9437188

commit v2 on v1

--- a/solution.py
+++ b/solution.py
@@ -25,7 +25,7 @@
 primal_step = 0.6
 dual_step = 0.8
 ball_radius = 12.0
-vmem_limit = 48 * 1024 * 1024
+vmem_limit = 32 * 1024 * 1024
 
 
 def split_table(matrix):
@@ -136,8 +136,9 @@
 
 def gradient_kernel(
     sky, meas_re, meas_im, mask, row_fh, row_fl, row_bh, row_bl,
-    lane_fh, lane_fl, lane_bh, lane_bl, twist, out, field, real_field,
+    lane_fh, lane_fl, lane_bh, lane_bl, twist, *rest,
 ):
+    out, field, real_field = rest[-3:]
     tiles, rows, _ = real_field.shape
     group = 4
 
@@ -217,11 +218,11 @@
     return pl.BlockSpec(array.shape, lambda c: (0,) * array.ndim)
 
 
-def channel_block(rows, columns):
-    return pl.BlockSpec((1, rows, columns), lambda c: (c, 0, 0))
-
-
-def data_gradient(sky_image, measured_real, measured_imaginary, sampling_mask):
+def channel_block(rows, columns, channel):
+    return pl.BlockSpec((1, rows, columns), lambda c: (channel, 0, 0))
+
+
+def data_gradient(sky_image, measured_real, measured_imaginary, sampling_mask, channel, after):
     channels, rows, columns = sky_image.shape
     tiles = columns // LANES
     row_forward, row_backward = row_tables(rows)
@@ -233,23 +234,25 @@
         + split_table(lane_backward)
         + [twist_table(tiles)]
     )
-    block = channel_block(rows, columns)
+    block = channel_block(rows, columns, channel)
     return pl.pallas_call(
         gradient_kernel,
         name="gradient",
-        grid=(channels,),
-        in_specs=[block] * 4 + [whole(table) for table in tables],
-        out_specs=block,
-        out_shape=jax.ShapeDtypeStruct(sky_image.shape, jnp.float32),
+        grid=(1,),
+        in_specs=[block] * 4
+        + [whole(table) for table in tables]
+        + [pl.BlockSpec(memory_space=pl.ANY)] * len(after),
+        out_specs=channel_block(rows, columns, 0),
+        out_shape=jax.ShapeDtypeStruct((1, rows, columns), jnp.float32),
         scratch_shapes=[
             pltpu.VMEM((tiles, rows, 2 * LANES), jnp.float32),
             pltpu.VMEM((tiles, rows, LANES), jnp.float32),
         ],
         compiler_params=pltpu.CompilerParams(vmem_limit_bytes=vmem_limit),
         cost_estimate=pl.CostEstimate(
-            flops=3 * 2 * channels * rows * columns * 1400, bytes_accessed=20 * channels * rows * columns, transcendentals=0
+            flops=3 * 2 * rows * columns * 1400, bytes_accessed=20 * rows * columns, transcendentals=0
         ),
-    )(sky_image, measured_real, measured_imaginary, sampling_mask, *tables)
+    )(sky_image, measured_real, measured_imaginary, sampling_mask, *tables, *after)
 
 
 def row_matrix(length):
@@ -285,9 +288,10 @@
 
 def wavelet_kernel(
     sky, gradient, coefficients, row_sh, row_sl, row_ah, row_al, col_sh, col_sl, col_ah, col_al,
-    next_image, analysed, turned,
+    *rest,
 ):
-    facets, _, rows, width = coefficients.shape
+    next_image, analysed, turned = rest[-3:]
+    facets, rows, width = coefficients.shape
     group = 4
 
     def primal(step, carry):
@@ -295,7 +299,7 @@
         for i in range(group):
             index = step * group + i
             parts.append(
-                jnp.concatenate([coefficients[index, 0], coefficients[(index + facets - 1) % facets, 0]], 1)
+                jnp.concatenate([coefficients[index], coefficients[(index + facets - 1) % facets]], 1)
             )
         prior = times_table(jnp.concatenate(parts, 0), col_sh, col_sl)
         prior = jnp.concatenate([prior[i * rows : (i + 1) * rows] for i in range(group)], 1)
@@ -318,15 +322,15 @@
             parts.append(jnp.concatenate([turned[index], turned[(index + 1) % facets]], 1))
         result = times_table(jnp.concatenate(parts, 0), col_ah, col_al)
         for i in range(group):
-            analysed[step * group + i, 0] = result[i * rows : (i + 1) * rows]
+            analysed[step * group + i] = result[i * rows : (i + 1) * rows]
         return carry
 
     lax.fori_loop(0, facets // group, columns, 0)
 
 
-def primal_step_and_analysis(sky_image, gradient, coefficients):
+def primal_step_and_analysis(sky_image, gradient, coefficients, channel, image):
     channels, rows, columns = sky_image.shape
-    facets, width = coefficients.shape[0], coefficients.shape[3]
+    facets, width = coefficients.shape[0], coefficients.shape[2]
     row_analysis = row_matrix(rows)
     col_analysis = facet_matrix(width)
     col_synthesis = np.concatenate([col_analysis[:width].T, col_analysis[width:].T], 0)
@@ -336,14 +340,17 @@
         + split_table(col_synthesis)
         + split_table(col_analysis)
     )
-    block = channel_block(rows, columns)
-    facet_block = pl.BlockSpec((facets, 1, rows, width), lambda c: (0, c, 0, 0))
+    block = channel_block(rows, columns, channel)
+    operands = [sky_image, gradient, coefficients] + tables
     return pl.pallas_call(
         wavelet_kernel,
         name="wavelet",
-        grid=(channels,),
-        in_specs=[block, block, facet_block] + [whole(table) for table in tables],
-        out_specs=[block, facet_block],
+        grid=(1,),
+        in_specs=[block, channel_block(rows, columns, 0), whole(coefficients)]
+        + [whole(table) for table in tables]
+        + [pl.BlockSpec(memory_space=pl.ANY)] * len(image),
+        out_specs=[block, whole(coefficients)],
+        input_output_aliases={len(operands): 0} if image else {},
         out_shape=[
             jax.ShapeDtypeStruct(sky_image.shape, jnp.float32),
             jax.ShapeDtypeStruct(coefficients.shape, jnp.float32),
@@ -351,49 +358,61 @@
         scratch_shapes=[pltpu.VMEM((facets, rows, width), jnp.float32)],
         compiler_params=pltpu.CompilerParams(vmem_limit_bytes=vmem_limit),
         cost_estimate=pl.CostEstimate(
-            flops=3 * 2 * channels * rows * columns * 700, bytes_accessed=20 * channels * rows * columns, transcendentals=0
+            flops=3 * 2 * rows * columns * 700, bytes_accessed=20 * rows * columns, transcendentals=0
         ),
-    )(sky_image, gradient, coefficients, *tables)
-
-
-def shrink_kernel(dual, update, out):
-    total = jnp.zeros(dual.shape[1:], jnp.float32)
-    for channel in range(dual.shape[0]):
-        lifted = dual[channel] + dual_step * update[channel]
-        out[channel] = lifted
-        total = total + lifted * lifted
+    )(*operands, *image)
+
+
+def shrink_kernel(dual, *refs):
+    updates, out = refs[:-1], refs[-1]
+    total = jnp.zeros(dual.shape[2:], jnp.float32)
+    for channel, update in enumerate(updates):
+        for source in range(dual.shape[0]):
+            lifted = dual[source, channel] + dual_step * update[source]
+            out[source, channel] = lifted
+            total = total + lifted * lifted
     factor = 1.0 / jnp.maximum(1.0, jnp.sqrt(total) / ball_radius)
-    for channel in range(dual.shape[0]):
-        out[channel] = out[channel] * factor
-
-
-def shrink(dual, update):
-    channels, rows, width = dual.shape
-    block = pl.BlockSpec((channels, 8, width), lambda r: (0, r, 0))
+    for channel in range(dual.shape[1]):
+        for source in range(dual.shape[0]):
+            out[source, channel] = out[source, channel] * factor
+
+
+def shrink(dual, updates):
+    sources, channels, rows, width = dual.shape
+    block = pl.BlockSpec((sources, channels, 8, width), lambda r: (0, 0, r, 0))
+    part = pl.BlockSpec((sources, 8, width), lambda r: (0, r, 0))
     return pl.pallas_call(
         shrink_kernel,
         name="shrink",
         grid=(rows // 8,),
-        in_specs=[block, block],
+        in_specs=[block] + [part] * channels,
         out_specs=block,
         out_shape=jax.ShapeDtypeStruct(dual.shape, jnp.float32),
-        compiler_params=pltpu.CompilerParams(vmem_limit_bytes=vmem_limit),
+        compiler_params=pltpu.CompilerParams(vmem_limit_bytes=12 * 1024 * 1024),
         cost_estimate=pl.CostEstimate(flops=5 * dual.size, bytes_accessed=12 * dual.size, transcendentals=0),
-    )(dual, update)
+    )(dual, *updates)
+
+
+def exchange(blocks):
+    return lax.all_to_all(blocks, "fac", split_axis=0, concat_axis=0, tiled=True)
 
 
 def shards(sky_image, measured_real, measured_imaginary, sampling_mask, dual_field):
     channels, rows, columns = sky_image.shape
     facets = lax.axis_size("fac")
-    local_dual = lax.all_to_all(dual_field, "fac", split_axis=0, concat_axis=0, tiled=True)
-    gradient = data_gradient(sky_image, measured_real, measured_imaginary, sampling_mask)
-    next_image, analysed = primal_step_and_analysis(
-        sky_image, gradient, local_dual.reshape(facets, channels, rows, columns // facets)
-    )
-    update = lax.all_to_all(
-        analysed.reshape(dual_field.shape), "fac", split_axis=0, concat_axis=0, tiled=True
-    )
-    return (next_image, shrink(dual_field, update))
+    dual = dual_field.reshape(facets, channels, rows, columns // facets)
+    local_dual = [exchange(dual[:, channel]) for channel in range(channels)]
+    image, updates, after = [], [], []
+    for channel in range(channels):
+        gradient = data_gradient(
+            sky_image, measured_real, measured_imaginary, sampling_mask, channel, after
+        )
+        next_image, analysed = primal_step_and_analysis(
+            sky_image, gradient, local_dual[channel], channel, image
+        )
+        updates.append(exchange(analysed))
+        image, after = [next_image], [analysed]
+    return (image[0], shrink(dual, updates).reshape(dual_field.shape))
 
 
 def solution(mesh):

time: 188 us -> 208 us (1.11)
  local copies, waits for them, and re-layouts: 1.78 us -> 30.2 us
  waiting for transfers between devices: 20 us -> 0.01 us
  blocking collectives: 75.4 us -> 87 us
  Pallas kernels: 81.1 us -> 77.3 us
  starting transfers between devices: 6.49 us -> 10.1 us
    unnamed x38 -> x88, local copies, waits for them, and re-layouts: 1.78 us -> 26.9 us
    all_to_all x1 -> x2, waiting for transfers between devices: 20 us -> 0.01 us  [exchange(): lax.all_to_all(blocks, 'fac', split_axis=0, concat_axis=0, tiled=True)]
    all_to_all x1 -> x2, blocking collectives: 75.4 us -> 87 us  [exchange(): lax.all_to_all(blocks, 'fac', split_axis=0, concat_axis=0, tiled=True)]
    all_to_all x1 -> x2, starting transfers between devices: 6.49 us -> 10.1 us  [exchange(): lax.all_to_all(blocks, 'fac', split_axis=0, concat_axis=0, tiled=True)]
    pallas_call x2 -> x4, Pallas kernels: 72.6 us -> 69.1 us  [the longest x2 45.6 us: data_gradient(): pl.pallas_call(gradient_kernel, name='gradient', grid=(1,), in_specs=[blo...]
    squeeze x0 -> x1, local copies, waits for them, and re-layouts: none -> 3.24 us  [shards(): local_dual = [exchange(dual[:, channel]) for channel in range(channels)]]
  transfers between devices with their start and end apart: 1 -> 2, of which waited for: 1 -> 0; matrix products, arithmetic and copies ran while one was open for 0% -> 0% of each run, Pallas kernels for 26% -> 34%
where the time goes in v2:
time: 208 us; the launch traced here: 206 us
  blocking collectives  87 us (42%)
  Pallas kernels  77.3 us (37%)
  local copies, waits for them, and re-layouts  30.2 us (15%)
  starting transfers between devices  10.1 us (5%)
    all_to_all x2, blocking collectives, exchange(): lax.all_to_all(blocks, 'fac', split_axis=0, concat_axis=0, tiled=True)  87 us
    pallas_call x2, Pallas kernels, data_gradient(): pl.pallas_call(gradient_kernel, name='gradient', grid=(1,), in_specs=[blo...  45.6 us
    unnamed x88, local copies, waits for them, and re-layouts  26.9 us
    pallas_call x2, Pallas kernels, primal_step_and_analysis(): pl.pallas_call(wavelet_kernel, name='wavelet', grid=(1,), in_specs=[block...  23.5 us
    all_to_all x2, starting transfers between devices, exchange(): lax.all_to_all(blocks, 'fac', split_axis=0, concat_axis=0, tiled=True)  10.1 us
    pallas_call x1, Pallas kernels, shrink(): pl.pallas_call(shrink_kernel, name='shrink', grid=(rows // 8,), in_specs=...  8.15 us
  transfers between devices with their start and end apart: 2, of which 0 were waited for; matrix products, arithmetic and copies ran while one was open for 0% of the time, Pallas kernels for 34%

profile of v2, /device:TPU:3, one launch (start us, length us, event | category | flops | bytes accessed | tf_op | source)
XLA Modules:
  0.0 205.6 jit_solution(16193284499882102631)
XLA Ops:
  0.6 3.2 %slice_bitcast_fusion = (f32[32,96,128]{2,1,0:T(8,128)}, f32[32,96,128]{2,1,0:T(8,128)S(1)}) fusion(f32[32,2,96,128]{3,2,1,0:T(8,128)} %bitcast.6), kind=kLoop, calls=%fused_computation | loop fusion | bytes 6291456 | tf_op jit(solution)/shard_map/squeeze | solution.py:404
  3.9 43.8 %all_to_all.20.coefficients = f32[32,96,128]{2,1,0:T(8,128)} all-to-all(f32[32,96,128]{2,1,0:T(8,128)S(1)} %get-tuple-element.11), channel_id=1, replica_groups=mesh['groups'=1,'fac'=32] {'fac'}, dimensions={0} | all-to-all | bytes 3145728 | tf_op jit(solution)/shard_map/all_to_all | solution.py:397
  47.6 4.1 %all-to-all-start.1 = ((f32[32,96,128]{2,1,0:T(8,128)}), f32[32,96,128]{2,1,0:T(8,128)}, u32[]{:S(2)}, u32[]{:S(2)}) async-start(f32[32,96,128]{2,1,0:T(8,128)} %get-tuple-element.10), calls=%async_computation.1 | async-start | bytes 3145728 | tf_op jit(solution)/shard_map/all_to_all | solution.py:397
  51.8 0.0 copy-done.12
  51.8 0.0 copy-done.13
  51.8 0.0 copy-done
  51.8 0.0 copy-start.2
  51.8 1.9 copy-done.2
  53.7 1.9 copy-done.4
  55.6 1.9 copy-done.6
  57.5 0.9 copy-done.14
  58.4 0.9 copy-done.16
  59.3 0.9 copy-done.18
  60.2 0.8 copy-done.28
  61.0 0.8 copy-done.30
  61.8 0.8 copy-done.32
  62.6 0.8 copy-done.34
  63.4 0.0 copy-start.26
  63.4 0.0 copy-start.36
  63.4 0.0 copy-start.38
  63.4 0.0 copy-start.40
  63.5 0.0 copy-start.42
  63.5 22.8 %gradient.2 = f32[1,96,4096]{2,1,0:T(8,128)S(1)} custom-call(f32[2,96,4096]{2,1,0:T(8,128)S(1)} %copy-done, f32[2,96,4096]{2,1,0:T(8,128)S(1)} %copy-done.2, f32[2,96,4096]{2,1,0:T(8,128)S(1)} %copy-done.4, s32[2,96,4096]{2,1,0:T(8,128)S(1)} %copy-done.6, bf16[192,96]{1,0:T(8,128)(2,1)S(1)} %copy-done.34, bf16[192,96]{1,0:T(8,128)(2,1)S(1)} %copy-done.32, ...), custom_call_target="tpu_custom_call" | custom-call | flops 3303014400 | bytes 7864320 | tf_op jit(solution)/shard_map/gradient/pallas_call | solution.py:238
  86.3 0.0 copy-done.10
  86.3 0.0 copy-done.20
  86.3 0.0 copy-done.22
  86.3 0.0 copy-done.24
  86.3 0.0 copy-done.26
  86.3 0.0 copy-done.36
  86.3 0.0 copy-done.38
  86.4 0.0 copy-done.40
  86.4 0.0 copy-done.42
  86.4 11.0 %wavelet.2 = (f32[2,96,4096]{2,1,0:T(8,128)}, f32[32,96,128]{2,1,0:T(8,128)S(1)}) custom-call(f32[2,96,4096]{2,1,0:T(8,128)S(1)} %copy-done, f32[1,96,4096]{2,1,0:T(8,128)S(1)} %gradient.2, f32[32,96,128]{2,1,0:T(8,128)S(1)} %copy-done.10, bf16[96,96]{1,0:T(8,128)(2,1)S(1)} %copy-done.42, bf16[96,96]{1,0:T(8,128)(2,1)S(1)} %copy-done.40, ...), custom_call_target="tpu_custom_call" | custom-call | flops 1651507200 | bytes 7864320 | tf_op jit(solution)/shard_map/wavelet/pallas_call | solution.py:345
  97.4 1.2 copy-done.8
  98.6 0.0 all-to-all-done.1.coefficients
  98.6 6.0 %all-to-all-start.2 = ((f32[32,96,128]{2,1,0:T(8,128)}), f32[32,96,128]{2,1,0:T(8,128)}, u32[]{:S(2)}, u32[]{:S(2)}) async-start(f32[32,96,128]{2,1,0:T(8,128)} %copy-done.8), calls=%async_computation.2 | async-start | bytes 3145728 | tf_op jit(solution)/shard_map/all_to_all | solution.py:397
  104.6 0.0 copy-start.3
  104.6 1.9 copy-done.3
  106.5 1.9 copy-done.5
  108.4 1.9 copy-done.7
  110.3 1.4 copy-done.9
  111.7 0.9 copy-done.15
  112.6 0.9 copy-done.17
  113.5 0.9 copy-done.19
  114.4 0.8 copy-done.29
  115.2 0.8 copy-done.31
  116.0 0.8 copy-done.33
  116.8 0.8 copy-done.35
  117.6 0.0 copy-start.37
  117.6 0.0 copy-start.39
  117.6 0.0 copy-start.41
  117.6 0.0 copy-start.43
  117.6 22.8 %gradient.3 = f32[1,96,4096]{2,1,0:T(8,128)S(1)} custom-call(f32[2,96,4096]{2,1,0:T(8,128)S(1)} %copy-done, f32[2,96,4096]{2,1,0:T(8,128)S(1)} %copy-done.3, f32[2,96,4096]{2,1,0:T(8,128)S(1)} %copy-done.5, s32[2,96,4096]{2,1,0:T(8,128)S(1)} %copy-done.7, bf16[192,96]{1,0:T(8,128)(2,1)S(1)} %copy-done.35, bf16[192,96]{1,0:T(8,128)(2,1)S(1)} %copy-done.33, ...), custom_call_target="tpu_custom_call" | custom-call | flops 3303014400 | bytes 7864320 | tf_op jit(solution)/shard_map/gradient/pallas_call | solution.py:238
  140.5 0.0 copy-done.21
  140.5 0.0 copy-done.23
  140.5 0.0 copy-done.25
  140.5 0.0 copy-done.27
  140.5 0.0 copy-done.37
  140.5 0.0 copy-done.39
  140.5 12.5 %wavelet.3 = (f32[2,96,4096]{2,1,0:T(8,128)}, f32[32,96,128]{2,1,0:T(8,128)S(1)}) custom-call(f32[2,96,4096]{2,1,0:T(8,128)S(1)} %copy-done, f32[1,96,4096]{2,1,0:T(8,128)S(1)} %gradient.3, f32[32,96,128]{2,1,0:T(8,128)} %all-to-all-done.1.coefficients, bf16[96,96]{1,0:T(8,128)(2,1)S(1)} %copy-done.43, ...), custom_call_target="tpu_custom_call", output_to_operand_aliasing={{0}: (11, {})} | custom-call | flops 1651507200 | bytes 7864320 | tf_op jit(solution)/shard_map/wavelet/pallas_call | solution.py:345
  153.0 1.1 copy-done.11
  154.2 0.0 all-to-all-done.2.refs_0_
  154.2 43.3 %all_to_all.21.refs_1_ = f32[32,96,128]{2,1,0:T(8,128)S(1)} all-to-all(f32[32,96,128]{2,1,0:T(8,128)} %copy-done.11), channel_id=1, replica_groups=mesh['groups'=1,'fac'=32] {'fac'}, dimensions={0} | all-to-all | bytes 3145728 | tf_op jit(solution)/shard_map/all_to_all | solution.py:397
  197.4 8.1 %shrink.1 = f32[32,2,96,128]{3,2,1,0:T(8,128)} custom-call(f32[32,2,96,128]{3,2,1,0:T(8,128)S(1)} %bitcast.7, f32[32,96,128]{2,1,0:T(8,128)} %all-to-all-done.2.refs_0_, f32[32,96,128]{2,1,0:T(8,128)S(1)} %all_to_all.21.refs_1_), custom_call_target="tpu_custom_call" | custom-call | flops 3932160 | bytes 9437184 | tf_op jit(solution)/shard_map/shrink/pallas_call | solution.py:384
  (36 shorter events, 0.1 us)
Async XLA Ops:
  3.9 47.9 %copy-start.12 = (f32[32,8,256]{2,1,0:T(8,128)S(1)}, f32[32,8,256]{2,1,0:T(8,128)}, u32[]{:S(2)}) copy-start(f32[32,8,256]{2,1,0:T(8,128)} %constant.42.clone.twist) | copy-start | bytes 786436
  3.9 47.9 %copy-start.13 = (bf16[256,256]{1,0:T(8,128)(2,1)S(1)}, bf16[256,256]{1,0:T(8,128)(2,1)}, u32[]{:S(2)}) copy-start(bf16[256,256]{1,0:T(8,128)(2,1)} %constant.41.clone.lane_bl) | copy-start | bytes 393220
  47.6 4.2 %copy-start = (f32[2,96,4096]{2,1,0:T(8,128)S(1)}, f32[2,96,4096]{2,1,0:T(8,128)}, u32[]{:S(2)}) copy-start(f32[2,96,4096]{2,1,0:T(8,128)} %sky.7) | copy-start | bytes 9437188
  47.6 50.9 %all-to-all-start.1 = ((f32[32,96,128]{2,1,0:T(8,128)}), f32[32,96,128]{2,1,0:T(8,128)}, u32[]{:S(2)}, u32[]{:S(2)}) async-start(f32[32,96,128]{2,1,0:T(8,128)} %get-tuple-element.10), calls=%async_computation.1 | async-start | bytes 3145728 | tf_op jit(solution)/shard_map/all_to_all | solution.py:397
  51.8 1.9 copy-start.2
  53.7 1.9 copy-start.4
  55.6 1.9 copy-start.6
  57.5 0.9 copy-start.14
  58.4 0.9 copy-start.16
  59.3 0.9 copy-start.18
  60.2 0.8 copy-start.28
  61.0 0.8 copy-start.30
  61.8 0.8 copy-start.32
  62.6 0.8 copy-start.34
  63.4 22.9 %copy-start.10 = (f32[32,96,128]{2,1,0:T(8,128)S(1)}, f32[32,96,128]{2,1,0:T(8,128)}, u32[]{:S(2)}) copy-start(f32[32,96,128]{2,1,0:T(8,128)} %all_to_all.20.coefficients) | copy-start | bytes 4718596
  63.4 22.9 %copy-start.20 = (bf16[256,128]{1,0:T(8,128)(2,1)S(1)}, bf16[256,128]{1,0:T(8,128)(2,1)}, u32[]{:S(2)}) copy-start(bf16[256,128]{1,0:T(8,128)(2,1)} %constant.50.clone.col_al) | copy-start | bytes 196612
  63.4 22.9 %copy-start.22 = (bf16[256,128]{1,0:T(8,128)(2,1)S(1)}, bf16[256,128]{1,0:T(8,128)(2,1)}, u32[]{:S(2)}) copy-start(bf16[256,128]{1,0:T(8,128)(2,1)} %constant.49.clone.col_ah) | copy-start | bytes 196612
  63.4 22.9 %copy-start.24 = (bf16[256,128]{1,0:T(8,128)(2,1)S(1)}, bf16[256,128]{1,0:T(8,128)(2,1)}, u32[]{:S(2)}) copy-start(bf16[256,128]{1,0:T(8,128)(2,1)} %constant.48.clone.col_sl) | copy-start | bytes 196612
  63.4 22.9 %copy-start.26 = (bf16[256,128]{1,0:T(8,128)(2,1)S(1)}, bf16[256,128]{1,0:T(8,128)(2,1)}, u32[]{:S(2)}) copy-start(bf16[256,128]{1,0:T(8,128)(2,1)} %constant.47.clone.col_sh) | copy-start | bytes 196612
  63.4 22.9 %copy-start.36 = (bf16[96,96]{1,0:T(8,128)(2,1)S(1)}, bf16[96,96]{1,0:T(8,128)(2,1)}, u32[]{:S(2)}) copy-start(bf16[96,96]{1,0:T(8,128)(2,1)} %constant.46.clone.row_al) | copy-start | bytes 55300
  63.4 22.9 %copy-start.38 = (bf16[96,96]{1,0:T(8,128)(2,1)S(1)}, bf16[96,96]{1,0:T(8,128)(2,1)}, u32[]{:S(2)}) copy-start(bf16[96,96]{1,0:T(8,128)(2,1)} %constant.45.clone.row_ah) | copy-start | bytes 55300
  63.4 22.9 %copy-start.40 = (bf16[96,96]{1,0:T(8,128)(2,1)S(1)}, bf16[96,96]{1,0:T(8,128)(2,1)}, u32[]{:S(2)}) copy-start(bf16[96,96]{1,0:T(8,128)(2,1)} %constant.44.clone.row_sl) | copy-start | bytes 55300
  63.5 22.9 %copy-start.42 = (bf16[96,96]{1,0:T(8,128)(2,1)S(1)}, bf16[96,96]{1,0:T(8,128)(2,1)}, u32[]{:S(2)}) copy-start(bf16[96,96]{1,0:T(8,128)(2,1)} %constant.43.clone.row_sh) | copy-start | bytes 55300
  97.4 1.2 copy-start.8
  98.6 55.6 %all-to-all-start.2 = ((f32[32,96,128]{2,1,0:T(8,128)}), f32[32,96,128]{2,1,0:T(8,128)}, u32[]{:S(2)}, u32[]{:S(2)}) async-start(f32[32,96,128]{2,1,0:T(8,128)} %copy-done.8), calls=%async_computation.2 | async-start | bytes 3145728 | tf_op jit(solution)/shard_map/all_to_all | solution.py:397
  104.6 1.9 copy-start.3
  106.5 1.9 copy-start.5
  108.4 1.9 copy-start.7
  110.3 1.4 copy-start.9
  111.7 0.9 copy-start.15
  112.6 0.9 copy-start.17
  113.5 0.9 copy-start.19
  114.4 0.8 copy-start.29
  115.2 0.8 copy-start.31
  116.0 0.8 copy-start.33
  116.8 0.8 copy-start.35
  117.6 22.9 %copy-start.21 = (bf16[256,128]{1,0:T(8,128)(2,1)S(1)}, bf16[256,128]{1,0:T(8,128)(2,1)}, u32[]{:S(2)}) copy-start(bf16[256,128]{1,0:T(8,128)(2,1)} %constant.50.clone.col_al) | copy-start | bytes 196612
  117.6 22.9 %copy-start.23 = (bf16[256,128]{1,0:T(8,128)(2,1)S(1)}, bf16[256,128]{1,0:T(8,128)(2,1)}, u32[]{:S(2)}) copy-start(bf16[256,128]{1,0:T(8,128)(2,1)} %constant.49.clone.col_ah) | copy-start | bytes 196612
  117.6 22.9 %copy-start.25 = (bf16[256,128]{1,0:T(8,128)(2,1)S(1)}, bf16[256,128]{1,0:T(8,128)(2,1)}, u32[]{:S(2)}) copy-start(bf16[256,128]{1,0:T(8,128)(2,1)} %constant.48.clone.col_sl) | copy-start | bytes 196612
  117.6 22.9 %copy-start.27 = (bf16[256,128]{1,0:T(8,128)(2,1)S(1)}, bf16[256,128]{1,0:T(8,128)(2,1)}, u32[]{:S(2)}) copy-start(bf16[256,128]{1,0:T(8,128)(2,1)} %constant.47.clone.col_sh) | copy-start | bytes 196612
  117.6 22.9 %copy-start.37 = (bf16[96,96]{1,0:T(8,128)(2,1)S(1)}, bf16[96,96]{1,0:T(8,128)(2,1)}, u32[]{:S(2)}) copy-start(bf16[96,96]{1,0:T(8,128)(2,1)} %constant.46.clone.row_al) | copy-start | bytes 55300
  117.6 22.9 %copy-start.39 = (bf16[96,96]{1,0:T(8,128)(2,1)S(1)}, bf16[96,96]{1,0:T(8,128)(2,1)}, u32[]{:S(2)}) copy-start(bf16[96,96]{1,0:T(8,128)(2,1)} %constant.45.clone.row_ah) | copy-start | bytes 55300
  117.6 22.9 %copy-start.41 = (bf16[96,96]{1,0:T(8,128)(2,1)S(1)}, bf16[96,96]{1,0:T(8,128)(2,1)}, u32[]{:S(2)}) copy-start(bf16[96,96]{1,0:T(8,128)(2,1)} %constant.44.clone.row_sl) | copy-start | bytes 55300
  117.6 22.9 %copy-start.43 = (bf16[96,96]{1,0:T(8,128)(2,1)S(1)}, bf16[96,96]{1,0:T(8,128)(2,1)}, u32[]{:S(2)}) copy-start(bf16[96,96]{1,0:T(8,128)(2,1)} %constant.43.clone.row_sh) | copy-start | bytes 55300
  153.0 1.1 copy-start.11
  154.2 43.3 %copy-start.1 = (f32[64,96,128]{2,1,0:T(8,128)S(1)}, f32[64,96,128]{2,1,0:T(8,128)}, u32[]{:S(2)}) copy-start(f32[64,96,128]{2,1,0:T(8,128)} %param.43) | copy-start | bytes 9437188

commit v3 on v1

--- a/solution.py
+++ b/solution.py
@@ -285,43 +285,106 @@
 
 def wavelet_kernel(
     sky, gradient, coefficients, row_sh, row_sl, row_ah, row_al, col_sh, col_sl, col_ah, col_al,
-    next_image, analysed, turned,
+    next_image, received, turned, analysed, send_sem, recv_sem, own_sem,
 ):
-    facets, _, rows, width = coefficients.shape
+    facets, channels, rows, width = coefficients.shape
     group = 4
-
-    def primal(step, carry):
-        parts = []
+    chunks = facets // group
+    me = lax.axis_index("fac")
+    mesh_id = pl.DeviceIdType.MESH
+
+    barrier = pltpu.get_barrier_semaphore()
+
+    def greet(shift, carry):
+        pl.semaphore_signal(
+            barrier, inc=1, device_id={"fac": (me + shift) % facets}, device_id_type=mesh_id
+        )
+        return carry
+
+    lax.fori_loop(1, facets, greet, 0)
+    pl.semaphore_wait(barrier, facets - 1)
+
+    def copy_to(facet, shift):
+        return pltpu.make_async_remote_copy(
+            src_ref=analysed.at[facet],
+            dst_ref=received.at[me],
+            send_sem=send_sem.at[shift],
+            recv_sem=recv_sem.at[shift],
+            device_id={"fac": facet},
+            device_id_type=mesh_id,
+        )
+
+    def chunk_at(step):
+        return (me // group + chunks // 2 + step) % chunks
+
+    def primal(step):
+        chunk = chunk_at(step)
+        here = pl.ds(pl.multiple_of(chunk * (group * width), group * width), group * width)
+        for channel in range(channels):
+            parts = []
+            for i in range(group):
+                index = chunk * group + i
+                parts.append(
+                    jnp.concatenate(
+                        [coefficients[index, channel], coefficients[(index + facets - 1) % facets, channel]], 1
+                    )
+                )
+            prior = times_table(jnp.concatenate(parts, 0), col_sh, col_sl)
+            prior = jnp.concatenate([prior[i * rows : (i + 1) * rows] for i in range(group)], 1)
+            prior = table_times(row_sh, row_sl, prior)
+            old = sky[channel, :, here]
+            new = jnp.maximum(old - primal_step * (gradient[channel, :, here] + prior), 0.0)
+            next_image[channel, :, here] = new
+            result = table_times(row_ah, row_al, 2.0 * new - old)
+            for i in range(group):
+                turned[chunk * group + i, channel] = result[:, i * width : (i + 1) * width]
+
+    def columns(step):
+        chunk = chunk_at(step)
+        for channel in range(channels):
+            parts = []
+            for i in range(group):
+                index = chunk * group + i
+                parts.append(
+                    jnp.concatenate([turned[index, channel], turned[(index + 1) % facets, channel]], 1)
+                )
+            result = times_table(jnp.concatenate(parts, 0), col_ah, col_al)
+            for i in range(group):
+                analysed[chunk * group + i, channel] = result[i * rows : (i + 1) * rows]
         for i in range(group):
-            index = step * group + i
-            parts.append(
-                jnp.concatenate([coefficients[index, 0], coefficients[(index + facets - 1) % facets, 0]], 1)
-            )
-        prior = times_table(jnp.concatenate(parts, 0), col_sh, col_sl)
-        prior = jnp.concatenate([prior[i * rows : (i + 1) * rows] for i in range(group)], 1)
-        prior = table_times(row_sh, row_sl, prior)
-        here = pl.ds(pl.multiple_of(step * (group * width), group * width), group * width)
-        old = sky[0, :, here]
-        new = jnp.maximum(old - primal_step * (gradient[0, :, here] + prior), 0.0)
-        next_image[0, :, here] = new
-        result = table_times(row_ah, row_al, 2.0 * new - old)
-        for i in range(group):
-            turned[step * group + i] = result[:, i * width : (i + 1) * width]
-        return carry
-
-    lax.fori_loop(0, facets // group, primal, 0)
-
-    def columns(step, carry):
-        parts = []
-        for i in range(group):
-            index = step * group + i
-            parts.append(jnp.concatenate([turned[index], turned[(index + 1) % facets]], 1))
-        result = times_table(jnp.concatenate(parts, 0), col_ah, col_al)
-        for i in range(group):
-            analysed[step * group + i, 0] = result[i * rows : (i + 1) * rows]
-        return carry
-
-    lax.fori_loop(0, facets // group, columns, 0)
+            facet = chunk * group + i
+
+            @pl.when(facet != me)
+            def _():
+                copy_to(facet, (facet - me + facets) % facets).start()
+
+    primal(0)
+
+    def both(step, carry):
+        primal(step)
+        columns(step - 1)
+        return carry
+
+    lax.fori_loop(1, chunks, both, 0)
+    columns(chunks - 1)
+    own = pltpu.make_async_copy(analysed.at[me], received.at[me], own_sem)
+    own.start()
+    own.wait()
+
+    def finish(shift, carry):
+        to = (me + shift) % facets
+        copy_to(to, shift).wait_send()
+        pltpu.make_async_remote_copy(
+            src_ref=analysed.at[to],
+            dst_ref=received.at[(me + facets - shift) % facets],
+            send_sem=send_sem.at[shift],
+            recv_sem=recv_sem.at[shift],
+            device_id={"fac": to},
+            device_id_type=mesh_id,
+        ).wait_recv()
+        return carry
+
+    lax.fori_loop(1, facets, finish, 0)
 
 
 def primal_step_and_analysis(sky_image, gradient, coefficients):
@@ -336,24 +399,31 @@
         + split_table(col_synthesis)
         + split_table(col_analysis)
     )
-    block = channel_block(rows, columns)
-    facet_block = pl.BlockSpec((facets, 1, rows, width), lambda c: (0, c, 0, 0))
+    operands = [sky_image, gradient, coefficients] + tables
+    vmem = pl.BlockSpec(memory_space=pltpu.VMEM)
     return pl.pallas_call(
         wavelet_kernel,
         name="wavelet",
-        grid=(channels,),
-        in_specs=[block, block, facet_block] + [whole(table) for table in tables],
-        out_specs=[block, facet_block],
+        in_specs=[vmem] * len(operands),
+        out_specs=[vmem, pl.BlockSpec(memory_space=pl.ANY)],
         out_shape=[
             jax.ShapeDtypeStruct(sky_image.shape, jnp.float32),
             jax.ShapeDtypeStruct(coefficients.shape, jnp.float32),
         ],
-        scratch_shapes=[pltpu.VMEM((facets, rows, width), jnp.float32)],
-        compiler_params=pltpu.CompilerParams(vmem_limit_bytes=vmem_limit),
+        scratch_shapes=[
+            pltpu.VMEM((facets, channels, rows, width), jnp.float32),
+            pltpu.VMEM((facets, channels, rows, width), jnp.float32),
+            pltpu.SemaphoreType.DMA((facets,)),
+            pltpu.SemaphoreType.DMA((facets,)),
+            pltpu.SemaphoreType.DMA,
+        ],
+        compiler_params=pltpu.CompilerParams(
+            vmem_limit_bytes=vmem_limit, collective_id=0, has_side_effects=True
+        ),
         cost_estimate=pl.CostEstimate(
             flops=3 * 2 * channels * rows * columns * 700, bytes_accessed=20 * channels * rows * columns, transcendentals=0
         ),
-    )(sky_image, gradient, coefficients, *tables)
+    )(*operands)
 
 
 def shrink_kernel(dual, update, out):
@@ -387,13 +457,10 @@
     facets = lax.axis_size("fac")
     local_dual = lax.all_to_all(dual_field, "fac", split_axis=0, concat_axis=0, tiled=True)
     gradient = data_gradient(sky_image, measured_real, measured_imaginary, sampling_mask)
-    next_image, analysed = primal_step_and_analysis(
+    next_image, update = primal_step_and_analysis(
         sky_image, gradient, local_dual.reshape(facets, channels, rows, columns // facets)
     )
-    update = lax.all_to_all(
-        analysed.reshape(dual_field.shape), "fac", split_axis=0, concat_axis=0, tiled=True
-    )
-    return (next_image, shrink(dual_field, update))
+    return (next_image, shrink(dual_field, update.reshape(dual_field.shape)))
 
 
 def solution(mesh):

time: 188 us -> 178 us (0.947)
  blocking collectives: 75.4 us -> 0 us
  Pallas kernels: 81.1 us -> 145 us
    all_to_all x1 -> x0, blocking collectives: 75.4 us -> none  [shards(): lax.all_to_all(analysed.reshape(dual_field.shape), 'fac', split_axis=0, c...]
    pallas_call x1, Pallas kernels: 24 us -> 88.5 us  [primal_step_and_analysis(): pl.pallas_call(wavelet_kernel, name='wavelet', in_specs=[vmem] * len(oper...]
  transfers between devices with their start and end apart: 1 -> 1, of which waited for: 1 -> 1; matrix products, arithmetic and copies ran while one was open for 0% -> 0% of each run, Pallas kernels for 26% -> 28%
where the time goes in v3:
time: 178 us; the launch traced here: 176 us
  Pallas kernels  145 us (81%)
  waiting for transfers between devices  20 us (11%)
  starting transfers between devices  6.49 us (4%)
  local copies, waits for them, and re-layouts  3.45 us (2%)
    pallas_call x1, Pallas kernels, primal_step_and_analysis(): pl.pallas_call(wavelet_kernel, name='wavelet', in_specs=[vmem] * len(oper...  88.5 us
    pallas_call x1, Pallas kernels, data_gradient(): pl.pallas_call(gradient_kernel, name='gradient', grid=(channels,), in_spe...  48.6 us
    all_to_all x1, waiting for transfers between devices, shards(): lax.all_to_all(dual_field, 'fac', split_axis=0, concat_axis=0, tiled=True)  20 us
    pallas_call x1, Pallas kernels, shrink(): pl.pallas_call(shrink_kernel, name='shrink', grid=(rows // 8,), in_specs=...  8.44 us
    all_to_all x1, starting transfers between devices, shards(): lax.all_to_all(dual_field, 'fac', split_axis=0, concat_axis=0, tiled=True)  6.49 us
  transfers between devices with their start and end apart: 1, of which 1 were waited for; matrix products, arithmetic and copies ran while one was open for 0% of the time, Pallas kernels for 28%

profile of v3, /device:TPU:3, one launch (start us, length us, event | category | flops | bytes accessed | tf_op | source)
XLA Modules:
  0.0 176.4 jit_solution(7082302943727957293)
XLA Ops:
  0.6 0.0 copy-start.1
  0.6 0.0 copy-start.2
  0.7 0.0 copy-start.3
  0.7 0.0 copy-start.4
  0.7 0.0 copy-start.5
  0.7 0.0 copy-start.10
  0.7 0.0 copy-start.11
  0.7 0.0 copy-start.12
  0.7 0.0 copy-start.13
  0.7 6.5 %all-to-all-start = ((f32[64,96,128]{2,1,0:T(8,128)}), f32[64,96,128]{2,1,0:T(8,128)}, u32[]{:S(2)}, u32[]{:S(2)}) async-start(f32[64,96,128]{2,1,0:T(8,128)} %dual.1), calls=%async_computation | async-start | bytes 6291456 | tf_op jit(solution)/shard_map/all_to_all | solution.py:458
  7.2 0.0 copy-done.1
  7.3 0.0 copy-done.2
  7.3 0.0 copy-done.3
  7.3 0.0 copy-done.4
  7.3 0.0 copy-done.5
  7.3 0.0 copy-done.10
  7.3 0.0 copy-done.11
  7.3 0.0 copy-done.12
  7.3 0.0 copy-done.13
  7.3 0.0 copy-start.6
  7.3 0.0 copy-start.7
  7.4 0.0 copy-start.8
  7.4 0.0 copy-start.9
  7.4 0.0 copy-start.14
  7.4 0.0 copy-start.15
  7.4 0.0 copy-start.16
  7.4 0.0 copy-start.17
  7.4 48.6 %gradient.1 = f32[2,96,4096]{2,1,0:T(8,128)S(1)} custom-call(f32[2,96,4096]{2,1,0:T(8,128)} %sky.3, f32[2,96,4096]{2,1,0:T(8,128)} %meas_re.1, f32[2,96,4096]{2,1,0:T(8,128)} %meas_im.1, s32[2,96,4096]{2,1,0:T(8,128)} %mask.1, bf16[192,96]{1,0:T(8,128)(2,1)S(1)} %copy-done.13, bf16[192,96]{1,0:T(8,128)(2,1)S(1)} %copy-done.12, ...), custom_call_target="tpu_custom_call" | custom-call | flops 6606028800 | bytes 15728640 | tf_op jit(solution)/shard_map/gradient/pallas_call | solution.py:237
  56.0 0.0 copy-start.18
  56.0 1.7 copy-done.18
  57.7 20.0 %all-to-all-done = f32[64,96,128]{2,1,0:T(8,128)} async-done(((f32[64,96,128]{2,1,0:T(8,128)}), f32[64,96,128]{2,1,0:T(8,128)}, u32[]{:S(2)}, u32[]{:S(2)}) %all-to-all-start) | async-done | bytes 3145760 | tf_op jit(solution)/shard_map/all_to_all | solution.py:458
  77.7 0.0 copy-done.6
  77.7 0.0 copy-done.7
  77.7 0.0 copy-done.8
  77.7 0.0 copy-done.9
  77.7 0.0 copy-done.14
  77.7 0.0 copy-done.15
  77.8 0.0 copy-done.16
  77.8 0.0 copy-done.17
  77.8 0.0 copy-start
  77.8 88.5 %wavelet.1 = (f32[2,96,4096]{2,1,0:T(8,128)S(1)}, f32[32,2,96,128]{3,2,1,0:T(8,128)}) custom-call(f32[2,96,4096]{2,1,0:T(8,128)} %sky.3, f32[2,96,4096]{2,1,0:T(8,128)} %copy-done.18, f32[32,2,96,128]{3,2,1,0:T(8,128)} %bitcast.coefficients, bf16[96,96]{1,0:T(8,128)(2,1)S(1)} %copy-done.17, bf16[96,96]{1,0:T(8,128)(2,1)S(1)} %copy-done.16, ...), custom_call_target="tpu_custom_call" | custom-call | flops 3303014400 | bytes 15728640 | tf_op jit(solution)/shard_map/wavelet/pallas_call | solution.py:404
  166.3 0.0 copy-done
  166.3 8.4 %shrink.1 = f32[64,96,128]{2,1,0:T(8,128)} custom-call(f32[64,96,128]{2,1,0:T(8,128)S(1)} %copy-done, f32[64,96,128]{2,1,0:T(8,128)} %bitcast.2), custom_call_target="tpu_custom_call" | custom-call | flops 3932160 | bytes 9437184 | tf_op jit(solution)/shard_map/shrink/pallas_call | solution.py:443
  174.7 1.7 copy.25
Async XLA Ops:
  0.6 6.6 %copy-start.1 = (f32[32,8,256]{2,1,0:T(8,128)S(1)}, f32[32,8,256]{2,1,0:T(8,128)}, u32[]{:S(2)}) copy-start(f32[32,8,256]{2,1,0:T(8,128)} %constant.42.clone.twist) | copy-start | bytes 786436
  0.6 6.6 %copy-start.2 = (bf16[256,256]{1,0:T(8,128)(2,1)S(1)}, bf16[256,256]{1,0:T(8,128)(2,1)}, u32[]{:S(2)}) copy-start(bf16[256,256]{1,0:T(8,128)(2,1)} %constant.41.clone.lane_bl) | copy-start | bytes 393220
  0.7 6.6 %copy-start.3 = (bf16[256,256]{1,0:T(8,128)(2,1)S(1)}, bf16[256,256]{1,0:T(8,128)(2,1)}, u32[]{:S(2)}) copy-start(bf16[256,256]{1,0:T(8,128)(2,1)} %constant.40.clone.lane_bh) | copy-start | bytes 393220
  0.7 6.6 %copy-start.4 = (bf16[256,256]{1,0:T(8,128)(2,1)S(1)}, bf16[256,256]{1,0:T(8,128)(2,1)}, u32[]{:S(2)}) copy-start(bf16[256,256]{1,0:T(8,128)(2,1)} %constant.39.clone.lane_fl) | copy-start | bytes 393220
  0.7 6.6 %copy-start.5 = (bf16[256,256]{1,0:T(8,128)(2,1)S(1)}, bf16[256,256]{1,0:T(8,128)(2,1)}, u32[]{:S(2)}) copy-start(bf16[256,256]{1,0:T(8,128)(2,1)} %constant.38.clone.lane_fh) | copy-start | bytes 393220
  0.7 6.6 %copy-start.10 = (bf16[96,192]{1,0:T(8,128)(2,1)S(1)}, bf16[96,192]{1,0:T(8,128)(2,1)}, u32[]{:S(2)}) copy-start(bf16[96,192]{1,0:T(8,128)(2,1)} %constant.37.clone.row_bl) | copy-start | bytes 110596
  0.7 6.6 %copy-start.11 = (bf16[96,192]{1,0:T(8,128)(2,1)S(1)}, bf16[96,192]{1,0:T(8,128)(2,1)}, u32[]{:S(2)}) copy-start(bf16[96,192]{1,0:T(8,128)(2,1)} %constant.36.clone.row_bh) | copy-start | bytes 110596
  0.7 6.6 %copy-start.12 = (bf16[192,96]{1,0:T(8,128)(2,1)S(1)}, bf16[192,96]{1,0:T(8,128)(2,1)}, u32[]{:S(2)}) copy-start(bf16[192,96]{1,0:T(8,128)(2,1)} %constant.35.clone.row_fl) | copy-start | bytes 110596
  0.7 6.6 %copy-start.13 = (bf16[192,96]{1,0:T(8,128)(2,1)S(1)}, bf16[192,96]{1,0:T(8,128)(2,1)}, u32[]{:S(2)}) copy-start(bf16[192,96]{1,0:T(8,128)(2,1)} %constant.34.clone.row_fh) | copy-start | bytes 110596
  0.7 77.0 %all-to-all-start = ((f32[64,96,128]{2,1,0:T(8,128)}), f32[64,96,128]{2,1,0:T(8,128)}, u32[]{:S(2)}, u32[]{:S(2)}) async-start(f32[64,96,128]{2,1,0:T(8,128)} %dual.1), calls=%async_computation | async-start | bytes 6291456 | tf_op jit(solution)/shard_map/all_to_all | solution.py:458
  7.3 70.4 %copy-start.6 = (bf16[256,128]{1,0:T(8,128)(2,1)S(1)}, bf16[256,128]{1,0:T(8,128)(2,1)}, u32[]{:S(2)}) copy-start(bf16[256,128]{1,0:T(8,128)(2,1)} %constant.50.clone.col_al) | copy-start | bytes 196612
  7.3 70.4 %copy-start.7 = (bf16[256,128]{1,0:T(8,128)(2,1)S(1)}, bf16[256,128]{1,0:T(8,128)(2,1)}, u32[]{:S(2)}) copy-start(bf16[256,128]{1,0:T(8,128)(2,1)} %constant.49.clone.col_ah) | copy-start | bytes 196612
  7.4 70.4 %copy-start.8 = (bf16[256,128]{1,0:T(8,128)(2,1)S(1)}, bf16[256,128]{1,0:T(8,128)(2,1)}, u32[]{:S(2)}) copy-start(bf16[256,128]{1,0:T(8,128)(2,1)} %constant.48.clone.col_sl) | copy-start | bytes 196612
  7.4 70.4 %copy-start.9 = (bf16[256,128]{1,0:T(8,128)(2,1)S(1)}, bf16[256,128]{1,0:T(8,128)(2,1)}, u32[]{:S(2)}) copy-start(bf16[256,128]{1,0:T(8,128)(2,1)} %constant.47.clone.col_sh) | copy-start | bytes 196612
  7.4 70.4 %copy-start.14 = (bf16[96,96]{1,0:T(8,128)(2,1)S(1)}, bf16[96,96]{1,0:T(8,128)(2,1)}, u32[]{:S(2)}) copy-start(bf16[96,96]{1,0:T(8,128)(2,1)} %constant.46.clone.row_al) | copy-start | bytes 55300
  7.4 70.3 %copy-start.15 = (bf16[96,96]{1,0:T(8,128)(2,1)S(1)}, bf16[96,96]{1,0:T(8,128)(2,1)}, u32[]{:S(2)}) copy-start(bf16[96,96]{1,0:T(8,128)(2,1)} %constant.45.clone.row_ah) | copy-start | bytes 55300
  7.4 70.3 %copy-start.16 = (bf16[96,96]{1,0:T(8,128)(2,1)S(1)}, bf16[96,96]{1,0:T(8,128)(2,1)}, u32[]{:S(2)}) copy-start(bf16[96,96]{1,0:T(8,128)(2,1)} %constant.44.clone.row_sl) | copy-start | bytes 55300
  7.4 70.3 %copy-start.17 = (bf16[96,96]{1,0:T(8,128)(2,1)S(1)}, bf16[96,96]{1,0:T(8,128)(2,1)}, u32[]{:S(2)}) copy-start(bf16[96,96]{1,0:T(8,128)(2,1)} %constant.43.clone.row_sh) | copy-start | bytes 55300
  56.0 1.7 copy-start.18
  77.8 88.5 %copy-start = (f32[64,96,128]{2,1,0:T(8,128)S(1)}, f32[64,96,128]{2,1,0:T(8,128)}, u32[]{:S(2)}) copy-start(f32[64,96,128]{2,1,0:T(8,128)} %dual.1) | copy-start | bytes 9437188

commit v4 on v1

--- a/solution.py
+++ b/solution.py
@@ -134,8 +134,8 @@
     return slabs
 
 
-def gradient_kernel(
-    sky, meas_re, meas_im, mask, row_fh, row_fl, row_bh, row_bl,
+def gradient_of(
+    channel, sky, meas_re, meas_im, mask, row_fh, row_fl, row_bh, row_bl,
     lane_fh, lane_fl, lane_bh, lane_bl, twist, out, field, real_field,
 ):
     tiles, rows, _ = real_field.shape
@@ -146,7 +146,7 @@
 
     def turn_in(step, carry):
         here = pl.ds(pl.multiple_of(step * 8, 8), 8)
-        for index, slab in enumerate(turn([sky[0, here, tile(t)] for t in range(tiles)])):
+        for index, slab in enumerate(turn([sky[channel, here, tile(t)] for t in range(tiles)])):
             real_field[index, here, :] = slab
         return carry
 
@@ -176,11 +176,11 @@
         spectrum = transform(points, -1.0)
         misfit = []
         for t in range(tiles):
-            weight = mask[0, here, tile(t)].astype(jnp.float32)
+            weight = mask[channel, here, tile(t)].astype(jnp.float32)
             misfit.append(
                 (
-                    weight * (spectrum[t][0] - meas_re[0, here, tile(t)]),
-                    weight * (spectrum[t][1] - meas_im[0, here, tile(t)]),
+                    weight * (spectrum[t][0] - meas_re[channel, here, tile(t)]),
+                    weight * (spectrum[t][1] - meas_im[channel, here, tile(t)]),
                 )
             )
         for t, (real, imag) in enumerate(transform(misfit, 1.0)):
@@ -207,49 +207,23 @@
     def turn_out(step, carry):
         here = pl.ds(pl.multiple_of(step * 8, 8), 8)
         for index, slab in enumerate(turn([real_field[t, here, :] for t in range(tiles)])):
-            out[0, here, tile(index)] = slab
+            out[here, tile(index)] = slab
         return carry
 
     lax.fori_loop(0, rows // 8, turn_out, 0)
 
 
-def whole(array):
-    return pl.BlockSpec(array.shape, lambda c: (0,) * array.ndim)
-
-
-def channel_block(rows, columns):
-    return pl.BlockSpec((1, rows, columns), lambda c: (c, 0, 0))
-
-
-def data_gradient(sky_image, measured_real, measured_imaginary, sampling_mask):
-    channels, rows, columns = sky_image.shape
+def gradient_tables(rows, columns):
     tiles = columns // LANES
     row_forward, row_backward = row_tables(rows)
     lane_forward, lane_backward = lane_tables(tiles)
-    tables = (
+    return (
         split_table(row_forward)
         + split_table(row_backward)
         + split_table(lane_forward)
         + split_table(lane_backward)
         + [twist_table(tiles)]
     )
-    block = channel_block(rows, columns)
-    return pl.pallas_call(
-        gradient_kernel,
-        name="gradient",
-        grid=(channels,),
-        in_specs=[block] * 4 + [whole(table) for table in tables],
-        out_specs=block,
-        out_shape=jax.ShapeDtypeStruct(sky_image.shape, jnp.float32),
-        scratch_shapes=[
-            pltpu.VMEM((tiles, rows, 2 * LANES), jnp.float32),
-            pltpu.VMEM((tiles, rows, LANES), jnp.float32),
-        ],
-        compiler_params=pltpu.CompilerParams(vmem_limit_bytes=vmem_limit),
-        cost_estimate=pl.CostEstimate(
-            flops=3 * 2 * channels * rows * columns * 1400, bytes_accessed=20 * channels * rows * columns, transcendentals=0
-        ),
-    )(sky_image, measured_real, measured_imaginary, sampling_mask, *tables)
 
 
 def row_matrix(length):
@@ -283,77 +257,210 @@
     return block[:, : 2 * width].T
 
 
-def wavelet_kernel(
-    sky, gradient, coefficients, row_sh, row_sl, row_ah, row_al, col_sh, col_sl, col_ah, col_al,
-    next_image, analysed, turned,
-):
-    facets, _, rows, width = coefficients.shape
+def step_kernel(*refs):
+    images_hbm, dual, fourier = refs[:4], refs[4], refs[5:14]
+    row_sh, row_sl, row_ah, row_al, col_sh, col_sl, col_ah, col_al = refs[14:22]
+    next_image, received = refs[22:24]
+    images = refs[24:28]
+    gradient, field, real_field, coefficients, turned, analysed = refs[28:34]
+    load_sem, first_send, first_recv, second_send, second_recv, own_sem = refs[34:]
+    sky = images[0]
+    facets, channels, rows, width = coefficients.shape
     group = 4
-
-    def primal(step, carry):
+    chunks = facets // group
+    me = lax.axis_index("fac")
+    mesh_id = pl.DeviceIdType.MESH
+
+    def load(index, channel):
+        return pltpu.make_async_copy(
+            images_hbm[index].at[channel], images[index].at[channel], load_sem.at[index, channel]
+        )
+
+    for channel in range(channels):
+        for index in range(4):
+            load(index, channel).start()
+
+    barrier = pltpu.get_barrier_semaphore()
+
+    def greet(shift, carry):
+        pl.semaphore_signal(
+            barrier, inc=1, device_id={"fac": (me + shift) % facets}, device_id_type=mesh_id
+        )
+        return carry
+
+    lax.fori_loop(1, facets, greet, 0)
+    pl.semaphore_wait(barrier, facets - 1)
+
+    def first_copy(channel, shift):
+        facet = (me + shift) % facets
+        return pltpu.make_async_remote_copy(
+            src_ref=dual.at[facet, channel],
+            dst_ref=coefficients.at[me, channel],
+            send_sem=first_send.at[channel, shift],
+            recv_sem=first_recv.at[channel, shift],
+            device_id={"fac": facet},
+            device_id_type=mesh_id,
+        )
+
+    def second_copy(channel, facet, shift):
+        return pltpu.make_async_remote_copy(
+            src_ref=analysed.at[facet, channel],
+            dst_ref=received.at[me, channel],
+            send_sem=second_send.at[channel, shift],
+            recv_sem=second_recv.at[channel, shift],
+            device_id={"fac": facet},
+            device_id_type=mesh_id,
+        )
+
+    for channel in range(channels):
+
+        def send(turn_index, carry, channel=channel):
+            odd = turn_index % 2
+            shift = odd * ((turn_index + 1) // 2) + (1 - odd) * (facets // 2 + turn_index // 2)
+            first_copy(channel, shift).start()
+            return carry
+
+        lax.fori_loop(0, facets - 1, send, 0)
+    own = pltpu.make_async_copy(dual.at[me], coefficients.at[me], own_sem.at[0])
+    own.start()
+    own.wait()
+
+    def chunk_at(step):
+        return (me // group + chunks // 2 + step) % chunks
+
+    def primal(channel, step):
+        chunk = chunk_at(step)
+        here = pl.ds(pl.multiple_of(chunk * (group * width), group * width), group * width)
         parts = []
         for i in range(group):
-            index = step * group + i
+            index = chunk * group + i
             parts.append(
-                jnp.concatenate([coefficients[index, 0], coefficients[(index + facets - 1) % facets, 0]], 1)
+                jnp.concatenate(
+                    [coefficients[index, channel], coefficients[(index + facets - 1) % facets, channel]], 1
+                )
             )
         prior = times_table(jnp.concatenate(parts, 0), col_sh, col_sl)
         prior = jnp.concatenate([prior[i * rows : (i + 1) * rows] for i in range(group)], 1)
         prior = table_times(row_sh, row_sl, prior)
-        here = pl.ds(pl.multiple_of(step * (group * width), group * width), group * width)
-        old = sky[0, :, here]
-        new = jnp.maximum(old - primal_step * (gradient[0, :, here] + prior), 0.0)
-        next_image[0, :, here] = new
+        old = sky[channel, :, here]
+        new = jnp.maximum(old - primal_step * (gradient[:, here] + prior), 0.0)
+        next_image[channel, :, here] = new
         result = table_times(row_ah, row_al, 2.0 * new - old)
         for i in range(group):
-            turned[step * group + i] = result[:, i * width : (i + 1) * width]
-        return carry
-
-    lax.fori_loop(0, facets // group, primal, 0)
-
-    def columns(step, carry):
+            turned[chunk * group + i] = result[:, i * width : (i + 1) * width]
+
+    def columns(channel, step):
+        chunk = chunk_at(step)
         parts = []
         for i in range(group):
-            index = step * group + i
+            index = chunk * group + i
             parts.append(jnp.concatenate([turned[index], turned[(index + 1) % facets]], 1))
         result = times_table(jnp.concatenate(parts, 0), col_ah, col_al)
         for i in range(group):
-            analysed[step * group + i, 0] = result[i * rows : (i + 1) * rows]
-        return carry
-
-    lax.fori_loop(0, facets // group, columns, 0)
-
-
-def primal_step_and_analysis(sky_image, gradient, coefficients):
+            facet = chunk * group + i
+            analysed[facet, channel] = result[i * rows : (i + 1) * rows]
+
+            @pl.when(facet != me)
+            def _():
+                second_copy(channel, facet, (facet - me + facets) % facets).start()
+
+    for channel in range(channels):
+        for index in range(4):
+            load(index, channel).wait()
+        gradient_of(channel, *images, *fourier, gradient, field, real_field)
+
+        def arrive(shift, carry, channel=channel):
+            pltpu.make_async_remote_copy(
+                src_ref=dual.at[(me + shift) % facets, channel],
+                dst_ref=coefficients.at[(me + facets - shift) % facets, channel],
+                send_sem=first_send.at[channel, shift],
+                recv_sem=first_recv.at[channel, shift],
+                device_id={"fac": (me + shift) % facets},
+                device_id_type=mesh_id,
+            ).wait_recv()
+            return carry
+
+        lax.fori_loop(1, facets, arrive, 0)
+        primal(channel, 0)
+
+        def both(step, carry, channel=channel):
+            primal(channel, step)
+            columns(channel, step - 1)
+            return carry
+
+        lax.fori_loop(1, chunks, both, 0)
+        columns(channel, chunks - 1)
+
+    own = pltpu.make_async_copy(analysed.at[me], received.at[me], own_sem.at[1])
+    own.start()
+    own.wait()
+
+    for channel in range(channels):
+
+        def finish(shift, carry, channel=channel):
+            to = (me + shift) % facets
+            first_copy(channel, shift).wait_send()
+            second_copy(channel, to, shift).wait_send()
+            pltpu.make_async_remote_copy(
+                src_ref=analysed.at[to, channel],
+                dst_ref=received.at[(me + facets - shift) % facets, channel],
+                send_sem=second_send.at[channel, shift],
+                recv_sem=second_recv.at[channel, shift],
+                device_id={"fac": to},
+                device_id_type=mesh_id,
+            ).wait_recv()
+            return carry
+
+        lax.fori_loop(1, facets, finish, 0)
+
+
+def primal_dual_step(sky_image, measured_real, measured_imaginary, sampling_mask, dual):
     channels, rows, columns = sky_image.shape
-    facets, width = coefficients.shape[0], coefficients.shape[3]
+    facets, width = dual.shape[0], dual.shape[3]
     row_analysis = row_matrix(rows)
     col_analysis = facet_matrix(width)
     col_synthesis = np.concatenate([col_analysis[:width].T, col_analysis[width:].T], 0)
     tables = (
-        split_table(row_analysis.T)
+        gradient_tables(rows, columns)
+        + split_table(row_analysis.T)
         + split_table(row_analysis)
         + split_table(col_synthesis)
         + split_table(col_analysis)
     )
-    block = channel_block(rows, columns)
-    facet_block = pl.BlockSpec((facets, 1, rows, width), lambda c: (0, c, 0, 0))
+    images = [sky_image, measured_real, measured_imaginary, sampling_mask]
+    vmem, anywhere = pl.BlockSpec(memory_space=pltpu.VMEM), pl.BlockSpec(memory_space=pl.ANY)
+    pairs = pltpu.SemaphoreType.DMA((channels, facets))
     return pl.pallas_call(
-        wavelet_kernel,
-        name="wavelet",
-        grid=(channels,),
-        in_specs=[block, block, facet_block] + [whole(table) for table in tables],
-        out_specs=[block, facet_block],
+        step_kernel,
+        name="step",
+        in_specs=[anywhere] * 5 + [vmem] * len(tables),
+        out_specs=[vmem, anywhere],
         out_shape=[
             jax.ShapeDtypeStruct(sky_image.shape, jnp.float32),
-            jax.ShapeDtypeStruct(coefficients.shape, jnp.float32),
+            jax.ShapeDtypeStruct(dual.shape, jnp.float32),
         ],
-        scratch_shapes=[pltpu.VMEM((facets, rows, width), jnp.float32)],
-        compiler_params=pltpu.CompilerParams(vmem_limit_bytes=vmem_limit),
+        scratch_shapes=[pltpu.VMEM(image.shape, image.dtype) for image in images]
+        + [
+            pltpu.VMEM((rows, columns), jnp.float32),
+            pltpu.VMEM((columns // LANES, rows, 2 * LANES), jnp.float32),
+            pltpu.VMEM((columns // LANES, rows, LANES), jnp.float32),
+            pltpu.VMEM(dual.shape, jnp.float32),
+            pltpu.VMEM((facets, rows, width), jnp.float32),
+            pltpu.VMEM(dual.shape, jnp.float32),
+            pltpu.SemaphoreType.DMA((4, channels)),
+            pairs,
+            pairs,
+            pairs,
+            pairs,
+            pltpu.SemaphoreType.DMA((2,)),
+        ],
+        compiler_params=pltpu.CompilerParams(
+            vmem_limit_bytes=vmem_limit, collective_id=0, has_side_effects=True
+        ),
         cost_estimate=pl.CostEstimate(
-            flops=3 * 2 * channels * rows * columns * 700, bytes_accessed=20 * channels * rows * columns, transcendentals=0
+            flops=3 * 2 * channels * rows * columns * 2100, bytes_accessed=32 * channels * rows * columns, transcendentals=0
         ),
-    )(sky_image, gradient, coefficients, *tables)
+    )(*images, dual, *tables)
 
 
 def shrink_kernel(dual, update, out):
@@ -369,11 +476,11 @@
 
 def shrink(dual, update):
     channels, rows, width = dual.shape
-    block = pl.BlockSpec((channels, 8, width), lambda r: (0, r, 0))
+    block = pl.BlockSpec((channels, 16, width), lambda r: (0, r, 0))
     return pl.pallas_call(
         shrink_kernel,
         name="shrink",
-        grid=(rows // 8,),
+        grid=(rows // 16,),
         in_specs=[block, block],
         out_specs=block,
         out_shape=jax.ShapeDtypeStruct(dual.shape, jnp.float32),
@@ -385,15 +492,14 @@
 def shards(sky_image, measured_real, measured_imaginary, sampling_mask, dual_field):
     channels, rows, columns = sky_image.shape
     facets = lax.axis_size("fac")
-    local_dual = lax.all_to_all(dual_field, "fac", split_axis=0, concat_axis=0, tiled=True)
-    gradient = data_gradient(sky_image, measured_real, measured_imaginary, sampling_mask)
-    next_image, analysed = primal_step_and_analysis(
-        sky_image, gradient, local_dual.reshape(facets, channels, rows, columns // facets)
+    next_image, update = primal_dual_step(
+        sky_image,
+        measured_real,
+        measured_imaginary,
+        sampling_mask,
+        dual_field.reshape(facets, channels, rows, columns // facets),
     )
-    update = lax.all_to_all(
-        analysed.reshape(dual_field.shape), "fac", split_axis=0, concat_axis=0, tiled=True
-    )
-    return (next_image, shrink(dual_field, update))
+    return (next_image, shrink(dual_field, update.reshape(dual_field.shape)))
 
 
 def solution(mesh):

time: 188 us -> 171 us (0.910)
  blocking collectives: 75.4 us -> 0 us
  Pallas kernels: 81.1 us -> 153 us
  waiting for transfers between devices: 20 us -> 0 us
  local copies, waits for them, and re-layouts: 1.78 us -> 15.7 us
  starting transfers between devices: 6.49 us -> 0 us
    all_to_all x1 -> x0, blocking collectives: 75.4 us -> none  [shards(): lax.all_to_all(analysed.reshape(dual_field.shape), 'fac', split_axis=0, c...]
    pallas_call x3 -> x2, Pallas kernels: 81.1 us -> 153 us  [the longest x1 148 us: primal_dual_step(): pl.pallas_call(step_kernel, name='step', in_specs=[anywhere] * 5 + [vmem]...]
    all_to_all x1 -> x0, waiting for transfers between devices: 20 us -> none  [shards(): lax.all_to_all(dual_field, 'fac', split_axis=0, concat_axis=0, tiled=True)]
    unnamed x38 -> x37, local copies, waits for them, and re-layouts: 1.78 us -> 15.7 us
    all_to_all x1 -> x0, starting transfers between devices: 6.49 us -> none  [shards(): lax.all_to_all(dual_field, 'fac', split_axis=0, concat_axis=0, tiled=True)]
  transfers between devices with their start and end apart: 1 -> 0, of which waited for: 1 -> 0; matrix products, arithmetic and copies ran while one was open for 0% -> 0% of each run, Pallas kernels for 26% -> 0%
where the time goes in v4:
time: 171 us; the launch traced here: 170 us
  Pallas kernels  153 us (89%)
  local copies, waits for them, and re-layouts  15.7 us (9%)
    pallas_call x1, Pallas kernels, primal_dual_step(): pl.pallas_call(step_kernel, name='step', in_specs=[anywhere] * 5 + [vmem]...  148 us
    unnamed x37, local copies, waits for them, and re-layouts  15.7 us
    pallas_call x1, Pallas kernels, shrink(): pl.pallas_call(shrink_kernel, name='shrink', grid=(rows // 16,), in_specs...  5.62 us

profile of v4, /device:TPU:3, one launch (start us, length us, event | category | flops | bytes accessed | tf_op | source)
XLA Modules:
  0.0 169.7 jit_solution(886204260201879767)
XLA Ops:
  0.6 0.0 copy-start.1
  0.6 0.9 copy-done.1
  1.6 0.0 copy-start.2
  1.6 0.9 copy-done.2
  2.5 0.0 copy-start.3
  2.5 0.9 copy-done.3
  3.4 0.0 copy-start.4
  3.4 0.9 copy-done.4
  4.3 0.0 copy-start.5
  4.3 0.9 copy-done.5
  5.2 0.0 copy-start.6
  5.2 0.8 copy-done.6
  6.0 0.0 copy-start.7
  6.0 0.8 copy-done.7
  6.9 0.0 copy-start.8
  6.9 0.8 copy-done.8
  7.7 0.0 copy-start.9
  7.7 0.8 copy-done.9
  8.6 0.0 copy-start.10
  8.6 0.8 copy-done.10
  9.4 0.0 copy-start.11
  9.4 0.8 copy-done.11
  10.2 0.0 copy-start.12
  10.2 0.8 copy-done.12
  11.0 0.0 copy-start.13
  11.0 0.8 copy-done.13
  11.8 0.0 copy-start.14
  11.8 0.7 copy-done.14
  12.5 0.0 copy-start.15
  12.5 0.7 copy-done.15
  13.2 0.0 copy-start.16
  13.2 0.7 copy-done.16
  14.0 0.0 copy-start.17
  14.0 0.7 copy-done.17
  14.7 0.0 copy-start
  14.7 147.7 %step.1 = (f32[2,96,4096]{2,1,0:T(8,128)S(1)}, f32[32,2,96,128]{3,2,1,0:T(8,128)}) custom-call(f32[2,96,4096]{2,1,0:T(8,128)} %refs_0_.1, f32[2,96,4096]{2,1,0:T(8,128)} %refs_1_.1, f32[2,96,4096]{2,1,0:T(8,128)} %refs_2_.1, s32[2,96,4096]{2,1,0:T(8,128)} %refs_3_.1, f32[32,2,96,128]{3,2,1,0:T(8,128)} %bitcast.2, bf16[192,96]{1,0:T(8,128)(2,1)S(1)} %copy-done.13, ...), custom_call_target="tpu_custom_call" | custom-call | flops 9909043200 | bytes 25165824 | tf_op jit(solution)/shard_map/step/pallas_call | solution.py:433
  162.4 0.0 copy-done
  162.4 5.6 %shrink.1 = f32[64,96,128]{2,1,0:T(8,128)} custom-call(f32[64,96,128]{2,1,0:T(8,128)S(1)} %copy-done, f32[64,96,128]{2,1,0:T(8,128)} %bitcast.3), custom_call_target="tpu_custom_call" | custom-call | flops 3932160 | bytes 9437184 | tf_op jit(solution)/shard_map/shrink/pallas_call | solution.py:480
  168.1 1.7 copy.25
Async XLA Ops:
  0.6 1.0 copy-start.1
  1.6 0.9 copy-start.2
  2.5 0.9 copy-start.3
  3.4 0.9 copy-start.4
  4.3 0.9 copy-start.5
  5.2 0.8 copy-start.6
  6.0 0.8 copy-start.7
  6.9 0.8 copy-start.8
  7.7 0.8 copy-start.9
  8.6 0.8 copy-start.10
  9.4 0.8 copy-start.11
  10.2 0.8 copy-start.12
  11.0 0.8 copy-start.13
  11.8 0.7 copy-start.14
  12.5 0.7 copy-start.15
  13.2 0.7 copy-start.16
  14.0 0.7 copy-start.17
  14.7 147.7 %copy-start = (f32[64,96,128]{2,1,0:T(8,128)S(1)}, f32[64,96,128]{2,1,0:T(8,128)}, u32[]{:S(2)}) copy-start(f32[64,96,128]{2,1,0:T(8,128)} %dual.1) | copy-start | bytes 9437188
